TPU v7x, 256 devices: a whole 4x4x8 slice. The times are simulated.
256 devices in a mesh: section: 2 (over core), dp: 16 (over z, x_hi), mp: 8 (over y, x_lo).
Axes of the slice: x: 4 (x_hi: 2, x_lo: 2; x = x_hi * 2 + x_lo), y: 4, z: 8, core: 2. Of those that a mesh axis runs over, the one named last changes fastest.
Arguments:
- token_ids: int32 [4, 512], replicated, may hold values from 0 to 65535
- next_ids: int32 [4, 512], replicated, may hold values from 0 to 65535
- embed_table: bfloat16 [65536, 7168], P(('section', 'dp'), 'mp'), may hold values from -6 to 6
- norm_gain: float32 [2, 7168], P('section'), may hold values from 0.5 to 1.5
- w_gate: bfloat16 [2, 7168, 1024], P('section', None, 'mp'), may hold values from -0.0625 to 0.0625
- w_up: bfloat16 [2, 7168, 1024], P('section', None, 'mp'), may hold values from -0.0625 to 0.0625
- w_down: bfloat16 [2, 1024, 7168], P('section', 'mp'), may hold values from -0.1875 to 0.1875
- mtp_gain: float32 [2, 7168], replicated, may hold values from 0.5 to 1.5
- main_cot: bfloat16 [4, 512, 7168], P(None, 'dp', 'mp'), may hold values from -6 to 6
- mtp_cot: bfloat16 [4, 512, 7168], P(None, 'dp', 'mp'), may hold values from -6 to 6
Outputs:
- embed_grad: bfloat16 [65536, 7168], P(('section', 'dp'), 'mp')
All inputs are finite; a program needn't handle non-finite values.
Results may differ from a plain program's by a relative error of at most 0.022.
Values may be sent and summed in bfloat16 or wider, within the bound.
A program may use at most 128 MiB of HBM per device.

v0:
```python
import jax
import jax.numpy as jnp
from jax import lax
from jax.sharding import PartitionSpec as P

EPS = 1e-06


def from_behind(value, axis, steps):
    count = lax.axis_size(axis)
    first, last = (max(0, -steps), min(count, count - steps))
    return lax.ppermute(value, axis, [(source, source + steps) for source in range(first, last)])


def inverse_rms(values):
    return lax.rsqrt(jnp.mean(values * values, axis=-1, keepdims=True) + EPS)


def norm_back(values, weight):
    inverse = inverse_rms(values)
    return inverse * weight - values * (inverse * inverse * inverse) * jnp.mean(
        values * weight, axis=-1, keepdims=True
    )


def mixed_inputs(hidden_rows, embedded, mtp_gain):
    hidden_f = hidden_rows.astype(jnp.float32)
    embedded_f = embedded.astype(jnp.float32)
    return (
        hidden_f * inverse_rms(hidden_f) * mtp_gain[0]
        + embedded_f * inverse_rms(embedded_f) * mtp_gain[1]
    ).astype(jnp.bfloat16)


def send_up(values):
    return from_behind(values, "section", -1)


def send_down(values):
    return from_behind(values, "section", 1)


def narrow(terms):
    return lax.psum(terms.astype(jnp.bfloat16), "mp").astype(jnp.float32)


def forward_block(stream, gain, gate_weight, up_weight, down_weight):
    whole = stream.astype(jnp.float32)
    normed = (whole * inverse_rms(whole) * gain).astype(jnp.bfloat16)
    gate_out = jnp.dot(normed, gate_weight, preferred_element_type=jnp.float32)
    up_out = jnp.dot(normed, up_weight, preferred_element_type=jnp.float32)
    hidden = (jax.nn.silu(gate_out) * up_out).astype(jnp.bfloat16)
    term = lax.optimization_barrier(
        jnp.dot(hidden, down_weight, preferred_element_type=jnp.float32).astype(jnp.bfloat16)
    )
    return (stream.astype(jnp.float32) + narrow(term.astype(jnp.float32))).astype(jnp.bfloat16)


def backward_block(stream, grad_out, gain, gate_weight, up_weight, down_weight):
    whole, grad_whole = (stream, grad_out)
    whole_f = whole.astype(jnp.float32)
    normed = (whole_f * inverse_rms(whole_f) * gain).astype(jnp.bfloat16)
    gate_out = jnp.dot(normed, gate_weight, preferred_element_type=jnp.float32)
    up_out = jnp.dot(normed, up_weight, preferred_element_type=jnp.float32)
    sigmoid_gate = jax.nn.sigmoid(gate_out)
    activated = gate_out * sigmoid_gate
    contract = (((1,), (1,)), ((), ()))
    grad_hidden = lax.dot_general(
        grad_whole, down_weight, contract, preferred_element_type=jnp.float32
    )
    grad_gate = (
        grad_hidden * up_out * sigmoid_gate * (1.0 + gate_out * (1.0 - sigmoid_gate))
    ).astype(jnp.bfloat16)
    grad_up = (grad_hidden * activated).astype(jnp.bfloat16)
    back = lax.dot_general(grad_gate, gate_weight, contract, preferred_element_type=jnp.float32)
    back = back + lax.dot_general(grad_up, up_weight, contract, preferred_element_type=jnp.float32)
    back = lax.optimization_barrier(back.astype(jnp.bfloat16)).astype(jnp.float32)
    grad_normed = narrow(back)
    return grad_out.astype(jnp.float32) + norm_back(stream.astype(jnp.float32), gain * grad_normed)


def body(
    token_ids, next_ids, embed_table, norm_gain, w_gate, w_up, w_down, mtp_gain, main_cot, mtp_cot
):
    sections = lax.axis_size("section")
    replicas = lax.axis_size("dp")
    section_index = lax.axis_index("section")
    replica = lax.axis_index("dp")
    mp_index = lax.axis_index("mp")
    batches = token_ids.shape[0]
    row_count = token_ids.shape[1] // replicas
    model_width = norm_gain.shape[1]
    vocab_rows = embed_table.shape[0]
    piece_width = embed_table.shape[1]
    is_first = section_index == 0
    is_last = section_index == sections - 1
    gain = norm_gain[0]
    gate_weight = w_gate[0]
    up_weight = w_up[0]
    down_weight = w_down[0]
    main_ids = token_ids.reshape(batches, replicas, row_count).transpose(1, 0, 2)
    after_ids = next_ids.reshape(batches, replicas, row_count).transpose(1, 0, 2)
    layout_ids = jnp.full((sections, replicas, batches, row_count), -1, jnp.int32)
    layout_ids = layout_ids.at[0].set(main_ids).at[sections - 1].set(after_ids)
    block_ids = layout_ids.reshape(-1)
    local_ids = block_ids - (section_index * replicas + replica) * vocab_rows
    inside = (local_ids >= 0) & (local_ids < vocab_rows)
    safe_ids = jnp.clip(local_ids, 0, vocab_rows - 1)
    picked = jnp.where(
        inside[:, None], jnp.take(embed_table, safe_ids, axis=0), jnp.zeros((), jnp.bfloat16)
    )
    own_piece = lax.psum_scatter(
        picked.astype(jnp.float32).astype(jnp.bfloat16),
        ("section", "dp"),
        scatter_dimension=0,
        tiled=True,
    ).astype(jnp.float32)
    own_piece = own_piece.astype(jnp.bfloat16).reshape(batches, row_count, piece_width)
    block_rows, main_full, mtp_full = (
        lax.all_gather(own_piece, "mp", axis=2, tiled=True),
        lax.all_gather(main_cot, "mp", axis=2, tiled=True),
        lax.all_gather(mtp_cot, "mp", axis=2, tiled=True),
    )
    local_rows = block_rows.shape[1]
    empty_rows = jnp.zeros((local_rows, model_width), jnp.bfloat16)
    empty_stack = jnp.zeros((batches, local_rows, model_width), jnp.bfloat16)
    ticks = batches + sections - 1

    def forward_tick(step_index, state_now):
        received, saved = state_now
        micro = step_index - section_index
        slot_index = jnp.clip(micro, 0, batches - 1)
        raw_rows = jnp.where(is_first, block_rows[slot_index], received)
        mixed = mixed_inputs(raw_rows, block_rows[slot_index], mtp_gain)
        block_in = jnp.where(is_last, mixed, raw_rows)
        result = forward_block(block_in, gain, gate_weight, up_weight, down_weight)
        active = (micro >= 0) & (micro < batches)
        saved = jnp.where(
            active, lax.dynamic_update_index_in_dim(saved, raw_rows, slot_index, 0), saved
        )
        return (send_down(result), saved)

    received, saved = lax.fori_loop(0, ticks, forward_tick, (empty_rows, empty_stack))

    def backward_tick(step_index, state_now):
        received, grads = state_now
        micro = step_index - (sections - 1 - section_index)
        slot_index = jnp.clip(micro, 0, batches - 1)
        raw_rows = saved[slot_index]
        embedded = block_rows[slot_index]
        mixed = mixed_inputs(raw_rows, embedded, mtp_gain)
        block_in = jnp.where(is_last, mixed, raw_rows)
        grad_out = jnp.where(is_last, mtp_full[slot_index], received)
        grad_in = backward_block(block_in, grad_out, gain, gate_weight, up_weight, down_weight)
        grad_main = main_full[slot_index].astype(jnp.float32) + norm_back(
            raw_rows.astype(jnp.float32), mtp_gain[0] * grad_in
        )
        grad_next = norm_back(embedded.astype(jnp.float32), mtp_gain[1] * grad_in)
        outgoing = jnp.where(is_last, grad_main, grad_in).astype(jnp.bfloat16)
        keeping = jnp.where(is_last, grad_next, grad_in).astype(jnp.bfloat16)
        active = (micro >= 0) & (micro < batches)
        grads = jnp.where(
            active, lax.dynamic_update_index_in_dim(grads, keeping, slot_index, 0), grads
        )
        return (send_up(outgoing), grads)

    received, grads = lax.fori_loop(0, ticks, backward_tick, (empty_rows, empty_stack))
    home = jnp.where(is_first | is_last, grads, jnp.zeros((), jnp.bfloat16))
    own_cols = lax.dynamic_slice_in_dim(home, mp_index * piece_width, piece_width, 2)
    everyone = lax.all_gather(
        own_cols.reshape(-1, piece_width), ("section", "dp"), axis=0, tiled=True
    )
    masked = jnp.where(inside[:, None], everyone.astype(jnp.float32), 0.0)
    table = jax.ops.segment_sum(masked, safe_ids, num_segments=vocab_rows)
    return table.astype(jnp.bfloat16)


def solution(mesh):
    return jax.shard_map(
        body,
        mesh=mesh,
        in_specs=(
            P(),
            P(),
            P(("section", "dp"), "mp"),
            P("section", None),
            P("section", None, "mp"),
            P("section", None, "mp"),
            P("section", "mp", None),
            P(),
            P(None, "dp", "mp"),
            P(None, "dp", "mp"),
        ),
        out_specs=P(("section", "dp"), "mp"),
        check_vma=False,
    )
```

profile of v0, /device:TPU:1, one launch (start us, length us, event | category | flops | bytes accessed | tf_op | source)
XLA Modules:
  0.0 1356.8 jit_solution(487868663507412958)
XLA Ops:
  9.4 22.3 %gather_fusion = bf16[4096,896]{1,0:T(8,128)(2,1)} fusion(bf16[2048,896]{1,0:T(8,128)(2,1)} %param.20, s32[4096]{0:T(1024)S(1)} %broadcast_clamp_fusion), kind=kCustom, calls=%fused_computation | custom fusion | bytes 14696448 | tf_op jit(solution)/shard_map/jit(_take)/gather | solution.py:110
  31.8 7.0 select_select_fusion
  40.1 140.3 %reduce-scatter.2.cloned.1.call-done = bf16[128,896]{1,0:T(8,128)(2,1)} async-done(((bf16[4096,896]{1,0:T(8,128)(2,1)}), bf16[128,896]{1,0:T(8,128)(2,1)}) %reduce-scatter.2.cloned.1.call-update) | async-done | bytes 229392 | tf_op jit(solution)/shard_map/reduce_scatter | solution.py:112
  180.4 51.0 %all-gather.7.cloned.1.call-done = bf16[4,32,7168]{2,1,0:T(8,128)(2,1)} async-done(((bf16[4,32,896]{2,1,0:T(8,128)(2,1)}), bf16[4,32,7168]{2,1,0:T(8,128)(2,1)}) %all-gather.7.cloned.1.call-update) | async-done | bytes 1835024 | tf_op jit(solution)/shard_map/all_gather | solution.py:120
  233.0 465.9 %while.34 = (s32[]{:T(128)}, bf16[32,7168]{1,0:T(8,128)(2,1)S(1)}, bf16[4,32,7168]{2,1,0:T(8,128)(2,1)}, pred[]{:T(512)}, pred[]{:T(512)}, /*index=5*/s32[]{:T(1...) while((s32[]{:T(128)}, bf16[32,7168]{1,0:T(8,128)(2,1)S(1)}, ...), condition=%wide.region_6.7_spmd, body=%wide.region_1.6_spmd.sunk | while | flops 183984224 | bytes 17697196 | solution.py:143
  234.2 2.1 fusion.125
  238.7 3.6 convolution_convert_fusion.2
  242.3 75.1 %all-reduce.3.cloned.1.call-done = bf16[32,7168]{1,0:T(8,128)(2,1)} async-done(((bf16[32,7168]{1,0:T(8,128)(2,1)}), bf16[32,7168]{1,0:T(8,128)(2,1)}) %all-reduce.3.cloned.1.call-update) | async-done | bytes 458768 | tf_op jit(solution)/shard_map/while/body/eval_jaxpr/psum | solution.py:44
  319.8 7.2 collective-permute-done
  328.2 2.1 fusion.125
  332.6 3.6 convolution_convert_fusion.2
  336.3 74.1 %all-reduce.3.cloned.1.call-done = bf16[32,7168]{1,0:T(8,128)(2,1)} async-done(((bf16[32,7168]{1,0:T(8,128)(2,1)}), bf16[32,7168]{1,0:T(8,128)(2,1)}) %all-reduce.3.cloned.1.call-update) | async-done | bytes 458768 | tf_op jit(solution)/shard_map/while/body/eval_jaxpr/psum | solution.py:44
  412.8 7.2 collective-permute-done
  421.2 2.1 fusion.125
  425.6 3.6 convolution_convert_fusion.2
  429.2 74.1 %all-reduce.3.cloned.1.call-done = bf16[32,7168]{1,0:T(8,128)(2,1)} async-done(((bf16[32,7168]{1,0:T(8,128)(2,1)}), bf16[32,7168]{1,0:T(8,128)(2,1)}) %all-reduce.3.cloned.1.call-update) | async-done | bytes 458768 | tf_op jit(solution)/shard_map/while/body/eval_jaxpr/psum | solution.py:44
  505.7 7.2 collective-permute-done
  514.1 2.1 fusion.125
  518.5 3.6 convolution_convert_fusion.2
  522.2 74.1 %all-reduce.3.cloned.1.call-done = bf16[32,7168]{1,0:T(8,128)(2,1)} async-done(((bf16[32,7168]{1,0:T(8,128)(2,1)}), bf16[32,7168]{1,0:T(8,128)(2,1)}) %all-reduce.3.cloned.1.call-update) | async-done | bytes 458768 | tf_op jit(solution)/shard_map/while/body/eval_jaxpr/psum | solution.py:44
  598.7 7.2 collective-permute-done
  607.1 2.1 fusion.125
  611.5 3.6 convolution_convert_fusion.2
  615.1 74.1 %all-reduce.3.cloned.1.call-done = bf16[32,7168]{1,0:T(8,128)(2,1)} async-done(((bf16[32,7168]{1,0:T(8,128)(2,1)}), bf16[32,7168]{1,0:T(8,128)(2,1)}) %all-reduce.3.cloned.1.call-update) | async-done | bytes 458768 | tf_op jit(solution)/shard_map/while/body/eval_jaxpr/psum | solution.py:44
  691.6 7.2 collective-permute-done
  700.3 503.2 %while.35 = (s32[]{:T(128)}, bf16[32,7168]{1,0:T(8,128)(2,1)S(1)}, bf16[4,32,7168]{2,1,0:T(8,128)(2,1)}, pred[]{:T(512)}, s32[]{:T(128)}, /*index=5*/bf16[4,32,7...) while((s32[]{:T(128)}, bf16[32,7168]{1,0:T(8,128)(2,1)S(1)}, ...), condition=%wide.region_15.16_spmd, body=%wide.region_7.15_spmd.sunk | while | flops 310182176 | bytes 39040636 | solution.py:167
  703.7 1.7 fusion.142
  705.9 2.6 fusion.144
  708.5 3.0 fusion.145
  711.6 74.0 %all-reduce.5.cloned.1.call-done = bf16[32,7168]{1,0:T(8,128)(2,1)} async-done(((bf16[32,7168]{1,0:T(8,128)(2,1)}), bf16[32,7168]{1,0:T(8,128)(2,1)}) %all-reduce.5.cloned.1.call-update) | async-done | bytes 458768 | tf_op jit(solution)/shard_map/while/body/eval_jaxpr/psum | solution.py:44
  786.9 2.2 fusion.147
  790.6 8.0 collective-permute-start.1
  798.6 2.3 fusion.149
  804.3 1.7 fusion.142
  806.5 2.6 fusion.144
  809.1 3.0 fusion.145
  812.2 74.0 %all-reduce.5.cloned.1.call-done = bf16[32,7168]{1,0:T(8,128)(2,1)} async-done(((bf16[32,7168]{1,0:T(8,128)(2,1)}), bf16[32,7168]{1,0:T(8,128)(2,1)}) %all-reduce.5.cloned.1.call-update) | async-done | bytes 458768 | tf_op jit(solution)/shard_map/while/body/eval_jaxpr/psum | solution.py:44
  887.5 2.2 fusion.147
  891.2 8.0 collective-permute-start.1
  899.2 2.3 fusion.149
  904.9 1.7 fusion.142
  907.1 2.6 fusion.144
  909.7 3.0 fusion.145
  912.8 74.1 %all-reduce.5.cloned.1.call-done = bf16[32,7168]{1,0:T(8,128)(2,1)} async-done(((bf16[32,7168]{1,0:T(8,128)(2,1)}), bf16[32,7168]{1,0:T(8,128)(2,1)}) %all-reduce.5.cloned.1.call-update) | async-done | bytes 458768 | tf_op jit(solution)/shard_map/while/body/eval_jaxpr/psum | solution.py:44
  988.2 2.2 fusion.147
  991.9 8.0 collective-permute-start.1
  999.8 2.3 fusion.149
  1005.6 1.7 fusion.142
  1007.8 2.6 fusion.144
  1010.4 3.0 fusion.145
  1013.5 74.1 %all-reduce.5.cloned.1.call-done = bf16[32,7168]{1,0:T(8,128)(2,1)} async-done(((bf16[32,7168]{1,0:T(8,128)(2,1)}), bf16[32,7168]{1,0:T(8,128)(2,1)}) %all-reduce.5.cloned.1.call-update) | async-done | bytes 458768 | tf_op jit(solution)/shard_map/while/body/eval_jaxpr/psum | solution.py:44
  1088.9 2.2 fusion.147
  1092.6 8.0 collective-permute-start.1
  1100.5 2.3 fusion.149
  1106.3 1.7 fusion.142
  1108.5 2.6 fusion.144
  1111.1 3.0 fusion.145
  1114.2 74.1 %all-reduce.5.cloned.1.call-done = bf16[32,7168]{1,0:T(8,128)(2,1)} async-done(((bf16[32,7168]{1,0:T(8,128)(2,1)}), bf16[32,7168]{1,0:T(8,128)(2,1)}) %all-reduce.5.cloned.1.call-update) | async-done | bytes 458768 | tf_op jit(solution)/shard_map/while/body/eval_jaxpr/psum | solution.py:44
  1189.5 2.2 fusion.147
  1193.2 8.0 collective-permute-start.1
  1201.2 2.3 fusion.149
  1205.2 99.1 %all-gather.11.cloned.1.call-done = bf16[4096,896]{1,0:T(8,128)(2,1)} async-done(((bf16[128,896]{1,0:T(8,128)(2,1)}), bf16[4096,896]{1,0:T(8,128)(2,1)}) %all-gather.11.cloned.1.call-update) | async-done | bytes 7340048 | tf_op jit(solution)/shard_map/all_gather | solution.py:170
  1304.3 39.7 %scatter_custom_fusion = f32[2048,896]{1,0:T(8,128)} fusion(s32[4096]{0:T(1024)S(1)} %reshape.272, bf16[4096,896]{1,0:T(8,128)(2,1)} %all-gather.11.cloned.1.call-done, f32[]{:T(128)} %constant.250.clone.1, pred[4096]{0:T(1024)(128)(4,1)S(1)} %and.43), kind=kCustom, calls=%fused_computation.107 | custom fusion | flops 11010048 | bytes 14685184 | tf_op jit(solution)/shard_map/scatter-add | solution.py:174
  1343.9 5.3 convert_element_type.213
  (184 shorter events, 70.6 us)
Async XLA Ops:
  7.4 173.0 %reduce-scatter.2.cloned.1.call-start = ((), (), s32[]{:S(2)}) async-start(), calls=%async_computation.2 | async-start | bytes 7569408 | tf_op jit(solution)/shard_map/reduce_scatter | solution.py:112
  38.8 194.1 %copy-start = (bf16[1,7168,128]{2,1,0:T(8,128)(2,1)S(1)}, bf16[1,7168,128]{2,1,0:T(8,128)(2,1)}, u32[]{:S(2)}) copy-start(bf16[1,7168,128]{2,1,0:T(8,128)(2,1)} %param.22) | copy-start | bytes 5505028
  38.8 194.1 %copy-start.3 = (f32[1,7168]{1,0:T(1,128)S(1)}, f32[1,7168]{1,0:T(1,128)}, u32[]{:S(2)}) copy-start(f32[1,7168]{1,0:T(1,128)} %param.21) | copy-start | bytes 86020
  38.8 194.1 %copy-start.4 = (f32[2,7168]{1,0:T(2,128)S(1)}, f32[2,7168]{1,0:T(2,128)}, u32[]{:S(2)}) copy-start(f32[2,7168]{1,0:T(2,128)} %param.25) | copy-start | bytes 172036
  38.9 141.6 %all-gather.5.cloned.1.call-start = ((), (), s32[]{:S(2)}) async-start(), calls=%async_computation.1 | async-start | bytes 2064384 | tf_op jit(solution)/shard_map/all_gather | solution.py:121
  39.4 141.0 %all-gather.9.cloned.1.call-start = ((), (), s32[]{:S(2)}) async-start(), calls=%async_computation.4 | async-start | bytes 2064384 | tf_op jit(solution)/shard_map/all_gather | solution.py:122
  40.0 191.4 %all-gather.7.cloned.1.call-start = ((), (), s32[]{:S(2)}) async-start(), calls=%async_computation.3 | async-start | bytes 2064384 | tf_op jit(solution)/shard_map/all_gather | solution.py:120
  233.0 84.4 %all-reduce.3.cloned.1.call-start = ((), (), s32[]{:S(2)}) async-start(), calls=%async_computation.6 | async-start | bytes 917504 | tf_op jit(solution)/shard_map/while/body/eval_jaxpr/psum | solution.py:44
  318.5 8.5 collective-permute-start
  327.0 83.4 %all-reduce.3.cloned.1.call-start = ((), (), s32[]{:S(2)}) async-start(), calls=%async_computation.6 | async-start | bytes 917504 | tf_op jit(solution)/shard_map/while/body/eval_jaxpr/psum | solution.py:44
  411.5 8.5 collective-permute-start
  420.0 83.4 %all-reduce.3.cloned.1.call-start = ((), (), s32[]{:S(2)}) async-start(), calls=%async_computation.6 | async-start | bytes 917504 | tf_op jit(solution)/shard_map/while/body/eval_jaxpr/psum | solution.py:44
  504.4 8.5 collective-permute-start
  512.9 83.4 %all-reduce.3.cloned.1.call-start = ((), (), s32[]{:S(2)}) async-start(), calls=%async_computation.6 | async-start | bytes 917504 | tf_op jit(solution)/shard_map/while/body/eval_jaxpr/psum | solution.py:44
  597.4 8.5 collective-permute-start
  605.9 83.3 %all-reduce.3.cloned.1.call-start = ((), (), s32[]{:S(2)}) async-start(), calls=%async_computation.6 | async-start | bytes 917504 | tf_op jit(solution)/shard_map/while/body/eval_jaxpr/psum | solution.py:44
  690.3 8.5 collective-permute-start
  700.3 5.2 copy-start.2
  700.3 85.3 %all-reduce.5.cloned.1.call-start = ((), (), s32[]{:S(2)}) async-start(), calls=%async_computation.7 | async-start | bytes 917504 | tf_op jit(solution)/shard_map/while/body/eval_jaxpr/psum | solution.py:44
  700.3 3.3 copy-start.1
  790.6 10.3 collective-permute-start.1
  800.9 5.2 copy-start.2
  800.9 85.4 %all-reduce.5.cloned.1.call-start = ((), (), s32[]{:S(2)}) async-start(), calls=%async_computation.7 | async-start | bytes 917504 | tf_op jit(solution)/shard_map/while/body/eval_jaxpr/psum | solution.py:44
  800.9 3.4 copy-start.1
  891.2 10.3 collective-permute-start.1
  901.5 5.2 copy-start.2
  901.5 85.4 %all-reduce.5.cloned.1.call-start = ((), (), s32[]{:S(2)}) async-start(), calls=%async_computation.7 | async-start | bytes 917504 | tf_op jit(solution)/shard_map/while/body/eval_jaxpr/psum | solution.py:44
  901.5 3.4 copy-start.1
  991.9 10.3 collective-permute-start.1
  1002.1 5.2 copy-start.2
  1002.1 85.4 %all-reduce.5.cloned.1.call-start = ((), (), s32[]{:S(2)}) async-start(), calls=%async_computation.7 | async-start | bytes 917504 | tf_op jit(solution)/shard_map/while/body/eval_jaxpr/psum | solution.py:44
  1002.2 3.4 copy-start.1
  1092.6 10.3 collective-permute-start.1
  1102.8 5.2 copy-start.2
  1102.8 85.4 %all-reduce.5.cloned.1.call-start = ((), (), s32[]{:S(2)}) async-start(), calls=%async_computation.7 | async-start | bytes 917504 | tf_op jit(solution)/shard_map/while/body/eval_jaxpr/psum | solution.py:44
  1102.9 3.4 copy-start.1
  1193.2 10.3 collective-permute-start.1
  1203.5 100.8 %all-gather.11.cloned.1.call-start = ((), (), s32[]{:S(2)}) async-start(), calls=%async_computation.5 | async-start | bytes 7569408 | tf_op jit(solution)/shard_map/all_gather | solution.py:170
Sparse Core Ops, SparseCore 0:
  38.9 141.3 reduce-scatter.1
  242.4 74.8 all-reduce.2
  336.4 73.9 all-reduce.2
  429.3 73.9 all-reduce.2
  522.3 73.9 all-reduce.2
  615.3 73.9 all-reduce.2
  711.7 73.8 all-reduce.4
  812.3 73.8 all-reduce.4
  912.9 73.9 all-reduce.4
  1013.6 73.9 all-reduce.4
  1114.3 73.9 all-reduce.4
  1207.1 97.0 all-gather.10
Sparse Core Ops, SparseCore 1:
  41.3 53.0 all-gather.4
  96.2 58.0 all-gather.8
  180.5 51.0 all-gather.6
where the time goes:
time: 1360 us
  waiting for transfers between devices  1070 us (79%)
  other arithmetic  138 us (10%)
  matrix products  59.6 us (4%)
  starting transfers between devices  46.5 us (3%)
  local copies, waits for them, and re-layouts  27.6 us (2%)
  between operations  15.2 us (1%)
    psum x10, waiting for transfers between devices, narrow(): return lax.psum(terms.astype(jnp.bfloat16), 'mp').astype(jnp.float32)  742 us
    reduce_scatter x1, waiting for transfers between devices, body(): lax.psum_scatter(picked.astype(jnp.float32).astype(jnp.bfloat16), ('secti...  140 us
    all_gather x1, waiting for transfers between devices, body(): lax.all_gather(own_cols.reshape(-1, piece_width), ('section', 'dp'), axis...  99.1 us
    all_gather x1, waiting for transfers between devices, body(): lax.all_gather(own_piece, 'mp', axis=2, tiled=True)  51 us
    ppermute x10, starting transfers between devices, from_behind(): lax.ppermute(value, axis, [(source, source + steps) for source in range(f...  46.2 us
    scatter-add x1, other arithmetic, body(): table = jax.ops.segment_sum(masked, safe_ids, num_segments=vocab_rows)  39.7 us
    ppermute x10, waiting for transfers between devices, from_behind(): lax.ppermute(value, axis, [(source, source + steps) for source in range(f...  35.8 us
    reduce_sum x25, other arithmetic, inverse_rms(): return lax.rsqrt(jnp.mean(values * values, axis=-1, keepdims=True) + EPS)  31.2 us
  transfers between devices with their start and end apart: 25, of which 18 were waited for; matrix products, arithmetic and copies ran while one was open for 1% of the time, Pallas kernels for 0%

commit v1 on v0

--- a/solution.py
+++ b/solution.py
@@ -1,6 +1,10 @@
+import functools
+
 import jax
 import jax.numpy as jnp
 from jax import lax
+from jax.experimental import pallas as pl
+from jax.experimental.pallas import tpu as pltpu
 from jax.sharding import PartitionSpec as P
 
 EPS = 1e-06
@@ -79,7 +83,7 @@
     return grad_out.astype(jnp.float32) + norm_back(stream.astype(jnp.float32), gain * grad_normed)
 
 
-def body(
+def dense_body(
     token_ids, next_ids, embed_table, norm_gain, w_gate, w_up, w_down, mtp_gain, main_cot, mtp_cot
 ):
     sections = lax.axis_size("section")
@@ -175,6 +179,760 @@
     return table.astype(jnp.bfloat16)
 
 
+MESH = pl.DeviceIdType.MESH
+SLOTS = 16
+BF = jnp.bfloat16
+F32 = jnp.float32
+COLS = (((1,), (1,)), ((), ()))
+ROWS = (((0,), (0,)), ((), ()))
+
+
+def dot(a, b):
+    return jnp.dot(a, b, preferred_element_type=F32)
+
+
+def dot_t(a, b):
+    return lax.dot_general(a, b, COLS, preferred_element_type=F32)
+
+
+def iota(shape, axis):
+    return lax.broadcasted_iota(jnp.int32, shape, axis)
+
+
+def greet(devices):
+    barrier = pltpu.get_barrier_semaphore()
+    for_all, count = devices
+
+    def signal(step, carry):
+        pl.semaphore_signal(barrier, inc=1, device_id=for_all(step), device_id_type=MESH)
+        return carry
+
+    lax.fori_loop(0, count, signal, 0)
+    pl.semaphore_wait(barrier, count)
+
+
+def remote(source, target, send_sem, recv_sem, device):
+    return pltpu.make_async_remote_copy(
+        src_ref=source,
+        dst_ref=target,
+        send_sem=send_sem,
+        recv_sem=recv_sem,
+        device_id=device,
+        device_id_type=MESH,
+    )
+
+
+def to_column(row):
+    count = row.shape[1]
+    eye = iota((count, count), 0) == iota((count, count), 1)
+    whole = jnp.broadcast_to(row, (count, count))
+    return jnp.sum(jnp.where(eye, whole, jnp.zeros_like(whole)), axis=1, keepdims=True)
+
+
+def to_row(column):
+    count = column.shape[0]
+    eye = iota((count, count), 0) == iota((count, count), 1)
+    whole = jnp.broadcast_to(column, (count, count))
+    return jnp.sum(jnp.where(eye, whole, jnp.zeros_like(whole)), axis=0, keepdims=True)
+
+
+def gather_kernel(
+    sections,
+    replicas,
+    parts,
+    ids_ref,
+    table_hbm,
+    gate_hbm,
+    up_hbm,
+    down_hbm,
+    rows_ref,
+    slot_ref,
+    lid_ref,
+    over_ref,
+    gu_out,
+    down_out,
+    table,
+    first,
+    rank,
+    lid,
+    onehot,
+    send,
+    recv,
+    table_sem,
+    local_sem,
+    send_sem,
+    recv_sem,
+    weight_local,
+    weight_send,
+    weight_recv,
+):
+    section = lax.axis_index("section")
+    replica = lax.axis_index("dp")
+    part = lax.axis_index("mp")
+    count = sections * replicas
+    me = section * replicas + replica
+    vocab_rows, width = table_hbm.shape
+    hidden = gate_hbm.shape[1]
+    tokens = ids_ref.shape[1]
+    load = pltpu.make_async_copy(table_hbm, table, table_sem)
+    load.start()
+
+    def column_peer(step):
+        other = lax.rem(me + 1 + step, count)
+        return other, (other // replicas, lax.rem(other, replicas), part)
+
+    def row_peer(step):
+        other = lax.rem(part + 1 + step, parts)
+        return other, (section, replica, other)
+
+    def any_peer(step):
+        column = column_peer(step)[1]
+        row = row_peer(step - (count - 1))[1]
+        is_column = step < count - 1
+        return tuple(jnp.where(is_column, a, b) for a, b in zip(column, row))
+
+    greet((any_peer, count - 1 + parts - 1))
+
+    def weight_pieces(source, slot):
+        features = pl.ds(pl.multiple_of(source * width, width), width)
+        return (
+            (gate_hbm.at[features, :], gu_out.at[slot, :, pl.ds(0, hidden)]),
+            (up_hbm.at[features, :], gu_out.at[slot, :, pl.ds(hidden, hidden)]),
+            (down_hbm.at[:, features], down_out.at[slot]),
+        )
+
+    def weight_copies(step):
+        other, device = row_peer(step)
+        return [
+            remote(a, b, weight_send.at[i, step], weight_recv.at[i, part], device)
+            for i, (a, b) in enumerate(weight_pieces(other, part))
+        ]
+
+    def weight_start(step, carry):
+        for copy in weight_copies(step):
+            copy.start()
+        return carry
+
+    lax.fori_loop(0, parts - 1, weight_start, 0)
+    own_weights = [
+        pltpu.make_async_copy(a, b, weight_local.at[i])
+        for i, (a, b) in enumerate(weight_pieces(part, part))
+    ]
+    for copy in own_weights:
+        copy.start()
+
+    earlier = iota((tokens, tokens), 0) < iota((tokens, tokens), 1)
+
+    def find_first(index, carry):
+        row = ids_ref[pl.ds(index, 1), :]
+        same = (to_column(row) == row) & earlier
+        seen = jnp.max(jnp.where(same, 1.0, 0.0), axis=0, keepdims=True)
+        first[pl.ds(index, 1), :] = 1.0 - seen
+        return carry
+
+    lax.fori_loop(0, count, find_first, 0)
+    ids = ids_ref[...]
+    shard = ids // vocab_rows
+    is_first = first[...]
+
+    def fill(index, most):
+        held = jnp.where(shard == index, is_first, 0.0)
+        return jnp.maximum(most, jnp.sum(held, axis=1, keepdims=True))
+
+    most = lax.fori_loop(0, count, fill, jnp.zeros((count, 1), F32))
+    over_ref[...] = jnp.broadcast_to(jnp.max(most, axis=0, keepdims=True), over_ref.shape)
+
+    mine = jnp.where(shard == me, is_first, 0.0)
+    triangle = jnp.where(earlier, 1.0, 0.0).astype(BF)
+    rank[...] = jnp.where(mine > 0.0, dot(mine.astype(BF), triangle), -1.0)
+
+    def find_lid(index, carry):
+        row = ids_ref[pl.ds(index, 1), :] - me * vocab_rows + 1
+        picks = rank[pl.ds(index, 1), :].astype(jnp.int32) == iota((SLOTS, tokens), 0)
+        found = jnp.sum(
+            jnp.where(picks, jnp.broadcast_to(row, picks.shape), 0), axis=1, keepdims=True
+        )
+        lid[pl.ds(pl.multiple_of(index * SLOTS, SLOTS), SLOTS), :] = jnp.broadcast_to(
+            found - 1, (SLOTS, tokens)
+        )
+        return carry
+
+    lax.fori_loop(0, count, find_lid, 0)
+    for block in range(count * SLOTS // tokens):
+        rows = pl.ds(block * tokens, tokens)
+        eye = iota((tokens, tokens), 0) == iota((tokens, tokens), 1)
+        row = jnp.sum(jnp.where(eye, lid[rows, :], 0), axis=0, keepdims=True)
+        lid_ref[:, rows] = jnp.broadcast_to(row, (8, tokens))
+
+    own_row = ids_ref[pl.ds(me, 1), :]
+    own_first = first[pl.ds(me, 1), :]
+    own_column = to_column(own_row)
+    shard_row = own_row // vocab_rows
+    first_column = to_column(own_first)
+    counted = (own_column // vocab_rows == shard_row) & earlier & (first_column > 0.0)
+    own_rank = jnp.sum(jnp.where(counted, 1, 0), axis=0, keepdims=True)
+    slot_row = shard_row * SLOTS + own_rank
+    leads = (own_column == own_row) & (own_first > 0.0)
+    slot_column = jnp.sum(
+        jnp.where(leads, jnp.broadcast_to(slot_row, leads.shape), 0), axis=1, keepdims=True
+    )
+    slot_ref[...] = jnp.broadcast_to(to_row(slot_column), (8, tokens))
+
+    load.wait()
+    group = tokens // SLOTS
+
+    def column_copy(step):
+        other, device = column_peer(step)
+        return remote(
+            send.at[other], recv.at[me], send_sem.at[step], recv_sem.at[me], device
+        )
+
+    def pick(block, carry):
+        for inner in range(group):
+            other = column_peer(block * group + inner)[0]
+            wanted = lid[pl.ds(pl.multiple_of(other * SLOTS, SLOTS), SLOTS), :]
+            for lane in range(vocab_rows // tokens):
+                hit = wanted == iota(wanted.shape, 1) + lane * tokens
+                onehot[pl.ds(inner * SLOTS, SLOTS), pl.ds(lane * tokens, tokens)] = jnp.where(
+                    hit, 1.0, 0.0
+                ).astype(BF)
+        found = dot(onehot[...], table[...]).astype(BF)
+        for inner in range(group):
+            step = block * group + inner
+            send[column_peer(step)[0]] = found[inner * SLOTS : (inner + 1) * SLOTS]
+
+            @pl.when(step < count - 1)
+            def _():
+                column_copy(step).start()
+
+        return carry
+
+    lax.fori_loop(0, count // group, pick, 0)
+    keep = pltpu.make_async_copy(send.at[me], recv.at[me], local_sem)
+    keep.start()
+    keep.wait()
+
+    def arrive(step, carry):
+        other, device = column_peer(step)
+        remote(send.at[me], recv.at[other], send_sem.at[step], recv_sem.at[other], device).wait_recv()
+        return carry
+
+    lax.fori_loop(0, count - 1, arrive, 0)
+    spread = jnp.where(slot_column == iota((tokens, count * SLOTS), 1), 1.0, 0.0).astype(BF)
+    rows_ref[...] = dot(spread, recv[...].reshape(count * SLOTS, width)).astype(BF)
+
+    def leave(step, carry):
+        column_copy(step).wait_send()
+        return carry
+
+    lax.fori_loop(0, count - 1, leave, 0)
+
+    def weight_wait(step, carry):
+        other, device = row_peer(step)
+        for i, (a, b) in enumerate(weight_pieces(other, other)):
+            remote(a, b, weight_send.at[i, step], weight_recv.at[i, other], device).wait_recv()
+        for copy in weight_copies(step):
+            copy.wait_send()
+        return carry
+
+    lax.fori_loop(0, parts - 1, weight_wait, 0)
+    for copy in own_weights:
+        copy.wait()
+
+
+def block_kernel(
+    parts,
+    rows_ref,
+    main_cot_ref,
+    mtp_cot_ref,
+    gu_ref,
+    down_ref,
+    gain_ref,
+    mtp_gain_ref,
+    grad_ref,
+    part_out,
+    part_in,
+    wide_in,
+    early_out,
+    early_in,
+    narrow_in,
+    wide_own,
+    narrow_own,
+    stat_out,
+    stat_in,
+    cross,
+    hold,
+    part_send,
+    part_recv,
+    early_send,
+    early_recv,
+    wide_send,
+    wide_recv,
+    narrow_send,
+    narrow_recv,
+    stat_send,
+    stat_recv,
+    cross_send,
+    cross_recv,
+):
+    section = lax.axis_index("section")
+    replica = lax.axis_index("dp")
+    part = lax.axis_index("mp")
+    tokens, width = rows_ref.shape
+    hidden = down_ref.shape[1]
+    model_width = parts * width
+    features = pl.ds(pl.multiple_of(part * width, width), width)
+
+    def peer(step):
+        other = lax.rem(part + 1 + step, parts)
+        return other, (section, replica, other)
+
+    def any_peer(step):
+        other = lax.rem(part + 1 + lax.rem(step, parts), parts)
+        there = jnp.where(step < parts - 1, section, 1 - section)
+        return (there, replica, other)
+
+    greet((any_peer, 2 * parts - 1))
+
+    gain = gain_ref[0:1, features]
+    gain_main = mtp_gain_ref[0:1, features]
+    gain_next = mtp_gain_ref[1:2, features]
+
+    def total(values):
+        return jnp.sum(values, axis=1, keepdims=True)
+
+    def inverse(sum_of_squares):
+        return lax.rsqrt(sum_of_squares / model_width + EPS)
+
+    def scatter_start(outs, ins, send_sem, recv_sem):
+        def one(step, carry):
+            other, device = peer(step)
+            remote(
+                outs.at[other], ins.at[part], send_sem.at[step], recv_sem.at[part], device
+            ).start()
+            return carry
+
+        lax.fori_loop(0, parts - 1, one, 0)
+
+    def spread_start(own, ins, send_sem, recv_sem):
+        def one(step, carry):
+            device = peer(step)[1]
+            remote(own, ins.at[part], send_sem.at[step], recv_sem.at[part], device).start()
+            return carry
+
+        lax.fori_loop(0, parts - 1, one, 0)
+
+    def arrive(own, ins, send_sem, recv_sem):
+        def one(step, carry):
+            other, device = peer(step)
+            copy = remote(own, ins.at[other], send_sem.at[step], recv_sem.at[other], device)
+            copy.wait_recv()
+            copy.wait_send()
+            return carry
+
+        lax.fori_loop(0, parts - 1, one, 0)
+
+    def fill_parts(outs, ins, values_of):
+        def one(step, carry):
+            other = lax.rem(part + 1 + step, parts)
+            outs[other] = values_of(other).astype(outs.dtype)
+            return carry
+
+        lax.fori_loop(0, parts, one, 0)
+        ins[part] = outs[part]
+
+    def summed(ins):
+        value = ins[0].astype(F32)
+        for index in range(1, parts):
+            value = value + ins[index].astype(F32)
+        return value
+
+    def put_stats(columns):
+        rows = [to_row(column) for column in columns]
+        rows = rows + [jnp.zeros_like(rows[0])] * (8 - len(rows))
+        stat_out[...] = jnp.concatenate(rows, axis=0)
+
+    def get_stats(slot, count):
+        value = stat_in[slot, 0]
+        for index in range(1, parts):
+            value = value + stat_in[slot, index]
+        return [to_column(value[index : index + 1, :]) for index in range(count)]
+
+    def share_stats(slot):
+        stat_in[slot, part] = stat_out[...]
+        spread_start(stat_out, stat_in.at[slot], stat_send, stat_recv.at[slot])
+
+    def gate_up(normed):
+        fill_parts(part_out, part_in, lambda index: dot(normed, gu_ref[index]))
+        scatter_start(part_out, part_in, part_send, part_recv)
+
+    def grad_hidden_start(grad):
+        fill_parts(early_out, early_in, lambda index: dot_t(grad, down_ref[index]))
+        scatter_start(early_out, early_in, early_send, early_recv)
+
+    def grad_hidden_wait():
+        arrive(early_out.at[0], early_in, early_send, early_recv)
+        return summed(early_in)
+
+    def backward(gate, up, grad_hidden):
+        sigmoid = jax.nn.sigmoid(gate)
+        grad_gate = grad_hidden * up * sigmoid * (1.0 + gate * (1.0 - sigmoid))
+        grad_up = grad_hidden * gate * sigmoid
+        wide_own[...] = jnp.concatenate([grad_gate, grad_up], axis=1).astype(BF)
+        wide_in[part] = wide_own[...]
+        spread_start(wide_own, wide_in, wide_send, wide_recv)
+        arrive(wide_own, wide_in, wide_send, wide_recv)
+        back = dot_t(wide_in[0], gu_ref[0])
+        for index in range(1, parts):
+            back = back + dot_t(wide_in[index], gu_ref[index])
+        return back * gain
+
+    @pl.when(section == 0)
+    def _():
+        rows = rows_ref[...].astype(F32)
+        put_stats([total(rows * rows)])
+        share_stats(0)
+        gate_up((rows * gain).astype(BF))
+        arrive(stat_out, stat_in.at[0], stat_send, stat_recv.at[0])
+        scale = inverse(get_stats(0, 1)[0])
+        arrive(part_out.at[0], part_in, part_send, part_recv)
+        whole = summed(part_in) * scale
+        hold[...] = whole
+        gate = whole[:, :hidden]
+        up = whole[:, hidden:]
+        narrow_own[...] = (gate * jax.nn.sigmoid(gate) * up).astype(BF)
+        narrow_in[part] = narrow_own[...]
+        spread_start(narrow_own, narrow_in, narrow_send, narrow_recv)
+        arrive(narrow_own, narrow_in, narrow_send, narrow_recv)
+        out = rows_ref[...].astype(F32)
+        for index in range(parts):
+            out = out + dot(narrow_in[index], down_ref[index])
+        cross[0] = out.astype(BF)
+        over = remote(
+            cross.at[0], cross.at[1], cross_send, cross_recv, (1 - section, replica, part)
+        )
+        over.start()
+        main = cross[0].astype(F32)
+        put_stats([total(main * main)])
+
+        def tell(step, carry):
+            other = lax.rem(part + step, parts)
+            remote(
+                stat_out,
+                stat_in.at[1, part],
+                stat_send.at[step],
+                stat_recv.at[1, part],
+                (1 - section, replica, other),
+            ).start()
+            return carry
+
+        lax.fori_loop(0, parts, tell, 0)
+
+        def told(step, carry):
+            other = lax.rem(part + step, parts)
+            remote(
+                stat_out,
+                stat_in.at[1, part],
+                stat_send.at[step],
+                stat_recv.at[1, part],
+                (1 - section, replica, other),
+            ).wait_send()
+            return carry
+
+        lax.fori_loop(0, parts, told, 0)
+        over.wait_send()
+        over.wait_recv()
+        grad = cross[1]
+        grad_hidden_start(grad)
+        grad_hidden = grad_hidden_wait()
+        whole = hold[...]
+        scaled = backward(whole[:, :hidden], whole[:, hidden:], grad_hidden)
+        rows = rows_ref[...].astype(F32)
+        put_stats([total(rows * scaled)])
+        share_stats(2)
+        arrive(stat_out, stat_in.at[2], stat_send, stat_recv.at[2])
+        mean = get_stats(2, 1)[0] / model_width
+        scale = inverse(get_stats(0, 1)[0])
+        result = grad.astype(F32) + scale * scaled - rows * (scale * scale * scale * mean)
+        grad_ref[...] = result.astype(BF)
+
+    @pl.when(section == 1)
+    def _():
+        rows = rows_ref[...].astype(F32)
+        put_stats([total(rows * rows)])
+        share_stats(0)
+        grad_hidden_start(mtp_cot_ref[...])
+        arrive(stat_out, stat_in.at[0], stat_send, stat_recv.at[0])
+        scale_next = inverse(get_stats(0, 1)[0])
+        grad_hidden = grad_hidden_wait()
+
+        def heard(index, carry):
+            remote(
+                stat_out,
+                stat_in.at[1, index],
+                stat_send.at[0],
+                stat_recv.at[1, index],
+                (1 - section, replica, part),
+            ).wait_recv()
+            return carry
+
+        lax.fori_loop(0, parts, heard, 0)
+        over = remote(
+            cross.at[0], cross.at[1], cross_send, cross_recv, (1 - section, replica, part)
+        )
+        over.wait_recv()
+        scale_main = inverse(get_stats(1, 1)[0])
+        main = cross[1].astype(F32)
+        mixed = (main * scale_main * gain_main + rows * scale_next * gain_next).astype(BF)
+        mixed = mixed.astype(F32)
+        put_stats([total(mixed * mixed)])
+        share_stats(2)
+        gate_up((mixed * gain).astype(BF))
+        arrive(stat_out, stat_in.at[2], stat_send, stat_recv.at[2])
+        scale = inverse(get_stats(2, 1)[0])
+        arrive(part_out.at[0], part_in, part_send, part_recv)
+        whole = summed(part_in) * scale
+        scaled = backward(whole[:, :hidden], whole[:, hidden:], grad_hidden)
+        cot = mtp_cot_ref[...].astype(F32)
+        next_weighted = rows * gain_next
+        main_weighted = main * gain_main
+        put_stats(
+            [
+                total(mixed * scaled),
+                total(next_weighted * scaled),
+                total(next_weighted * mixed),
+                total(next_weighted * cot),
+                total(main_weighted * scaled),
+                total(main_weighted * mixed),
+                total(main_weighted * cot),
+            ]
+        )
+        share_stats(3)
+        arrive(stat_out, stat_in.at[3], stat_send, stat_recv.at[3])
+        s1, s2, s3, s4, s5, s6, s7 = get_stats(3, 7)
+        slope = scale * scale * scale * (s1 / model_width)
+        grad_mixed = cot + scale * scaled - mixed * slope
+        mean_next = (s4 + scale * s2 - slope * s3) / model_width
+        mean_main = (s7 + scale * s5 - slope * s6) / model_width
+        grad_main = (
+            main_cot_ref[...].astype(F32)
+            + scale_main * (gain_main * grad_mixed)
+            - main * (scale_main * scale_main * scale_main * mean_main)
+        )
+        cross[0] = grad_main.astype(BF)
+        over.start()
+        grad_next = scale_next * (gain_next * grad_mixed) - rows * (
+            scale_next * scale_next * scale_next * mean_next
+        )
+        grad_ref[...] = grad_next.astype(BF)
+        over.wait_send()
+
+
+def scatter_kernel(
+    sections, replicas, grad_ref, slot_ref, out_ref, send, send_sem, recv_sem, local_sem
+):
+    section = lax.axis_index("section")
+    replica = lax.axis_index("dp")
+    part = lax.axis_index("mp")
+    count = sections * replicas
+    me = section * replicas + replica
+    tokens, width = grad_ref.shape
+
+    def peer(step):
+        other = lax.rem(me + 1 + step, count)
+        return other, (other // replicas, lax.rem(other, replicas), part)
+
+    greet((lambda step: peer(step)[1], count - 1))
+    slots = count * SLOTS
+    spread = jnp.where(slot_ref[0:1, :] == iota((slots, tokens), 0), 1.0, 0.0).astype(BF)
+    send[...] = dot(spread, grad_ref[...]).astype(BF).reshape(count, SLOTS, width)
+
+    def copy(step):
+        other, device = peer(step)
+        return remote(
+            send.at[other], out_ref.at[me], send_sem.at[step], recv_sem.at[me], device
+        )
+
+    def start(step, carry):
+        copy(step).start()
+        return carry
+
+    lax.fori_loop(0, count - 1, start, 0)
+    keep = pltpu.make_async_copy(send.at[me], out_ref.at[me], local_sem)
+    keep.start()
+    keep.wait()
+
+    def arrive(step, carry):
+        other, device = peer(step)
+        remote(
+            send.at[me], out_ref.at[other], send_sem.at[step], recv_sem.at[other], device
+        ).wait_recv()
+        copy(step).wait_send()
+        return carry
+
+    lax.fori_loop(0, count - 1, arrive, 0)
+
+
+def place_kernel(lid_ref, sums_ref, out_ref):
+    rows = out_ref.shape[0]
+    slots = sums_ref.shape[0]
+    base = pl.program_id(0) * rows
+    hit = lid_ref[0:1, :] == iota((rows, slots), 0) + base
+    out_ref[...] = dot(jnp.where(hit, 1.0, 0.0).astype(BF), sums_ref[...]).astype(BF)
+
+
+def vmem():
+    return pl.BlockSpec(memory_space=pltpu.VMEM)
+
+
+def anywhere():
+    return pl.BlockSpec(memory_space=pl.ANY)
+
+
+def dma(*shape):
+    return pltpu.SemaphoreType.DMA(shape)
+
+
+def params(collective_id):
+    return pltpu.CompilerParams(
+        collective_id=collective_id, has_side_effects=True, vmem_limit_bytes=56 << 20
+    )
+
+
+def fast_body(
+    token_ids, next_ids, embed_table, norm_gain, w_gate, w_up, w_down, mtp_gain, main_cot, mtp_cot
+):
+    sections = lax.axis_size("section")
+    replicas = lax.axis_size("dp")
+    parts = lax.axis_size("mp")
+    count = sections * replicas
+    batches = token_ids.shape[0]
+    row_count = token_ids.shape[1] // replicas
+    tokens = batches * row_count
+    vocab_rows, width = embed_table.shape
+    hidden = w_gate.shape[2]
+    ids = jnp.stack([token_ids, next_ids]).reshape(sections, batches, replicas, row_count)
+    ids = ids.transpose(0, 2, 1, 3).reshape(count, tokens)
+    slots = count * SLOTS
+    rows, slot_row, lid_row, most, gate_up, down = pl.pallas_call(
+        functools.partial(gather_kernel, sections, replicas, parts),
+        out_shape=(
+            jax.ShapeDtypeStruct((tokens, width), BF),
+            jax.ShapeDtypeStruct((8, tokens), jnp.int32),
+            jax.ShapeDtypeStruct((8, slots), jnp.int32),
+            jax.ShapeDtypeStruct((8, 128), F32),
+            jax.ShapeDtypeStruct((parts, width, 2 * hidden), BF),
+            jax.ShapeDtypeStruct((parts, hidden, width), BF),
+        ),
+        in_specs=[vmem()] + [anywhere()] * 4,
+        out_specs=(vmem(), vmem(), vmem(), vmem(), anywhere(), anywhere()),
+        scratch_shapes=[
+            pltpu.VMEM((vocab_rows, width), BF),
+            pltpu.VMEM((count, tokens), F32),
+            pltpu.VMEM((count, tokens), F32),
+            pltpu.VMEM((slots, tokens), jnp.int32),
+            pltpu.VMEM((tokens, vocab_rows), BF),
+            pltpu.VMEM((count, SLOTS, width), BF),
+            pltpu.VMEM((count, SLOTS, width), BF),
+            pltpu.SemaphoreType.DMA,
+            pltpu.SemaphoreType.DMA,
+            dma(count),
+            dma(count),
+            dma(3),
+            dma(3, parts),
+            dma(3, parts),
+        ],
+        compiler_params=params(0),
+        name="gather_rows",
+    )(ids, embed_table, w_gate[0], w_up[0], w_down[0])
+    grads = pl.pallas_call(
+        functools.partial(block_kernel, parts),
+        out_shape=jax.ShapeDtypeStruct((tokens, width), BF),
+        in_specs=[vmem()] * 7,
+        out_specs=vmem(),
+        scratch_shapes=[
+            pltpu.VMEM((parts, tokens, 2 * hidden), BF),
+            pltpu.VMEM((parts, tokens, 2 * hidden), BF),
+            pltpu.VMEM((parts, tokens, 2 * hidden), BF),
+            pltpu.VMEM((parts, tokens, hidden), BF),
+            pltpu.VMEM((parts, tokens, hidden), BF),
+            pltpu.VMEM((parts, tokens, hidden), BF),
+            pltpu.VMEM((tokens, 2 * hidden), BF),
+            pltpu.VMEM((tokens, hidden), BF),
+            pltpu.VMEM((8, tokens), F32),
+            pltpu.VMEM((4, parts, 8, tokens), F32),
+            pltpu.VMEM((2, tokens, width), BF),
+            pltpu.VMEM((tokens, 2 * hidden), F32),
+            dma(parts),
+            dma(parts),
+            dma(parts),
+            dma(parts),
+            dma(parts),
+            dma(parts),
+            dma(parts),
+            dma(parts),
+            dma(parts),
+            dma(4, parts),
+            pltpu.SemaphoreType.DMA,
+            pltpu.SemaphoreType.DMA,
+        ],
+        compiler_params=params(1),
+        name="blocks",
+    )(
+        rows,
+        main_cot.reshape(tokens, width),
+        mtp_cot.reshape(tokens, width),
+        gate_up,
+        down,
+        norm_gain,
+        mtp_gain,
+    )
+    sums = pl.pallas_call(
+        functools.partial(scatter_kernel, sections, replicas),
+        out_shape=jax.ShapeDtypeStruct((count, SLOTS, width), BF),
+        in_specs=[vmem()] * 2,
+        out_specs=vmem(),
+        scratch_shapes=[
+            pltpu.VMEM((count, SLOTS, width), BF),
+            dma(count),
+            dma(count),
+            pltpu.SemaphoreType.DMA,
+        ],
+        compiler_params=params(2),
+        name="scatter_rows",
+    )(grads, slot_row)
+    return most[0, 0], lid_row, sums.reshape(slots, width)
+
+
+def place(lid_row, sums, vocab_rows):
+    slots, width = sums.shape
+    block = vocab_rows // 8
+    return pl.pallas_call(
+        place_kernel,
+        grid=(vocab_rows // block,),
+        out_shape=jax.ShapeDtypeStruct((vocab_rows, width), BF),
+        in_specs=[
+            pl.BlockSpec((8, slots), lambda i: (0, 0)),
+            pl.BlockSpec((slots, width), lambda i: (0, 0)),
+        ],
+        out_specs=pl.BlockSpec((block, width), lambda i: (i, 0)),
+        name="place_rows",
+    )(lid_row, sums)
+
+
+def body(*arguments):
+    most, lid_row, sums = fast_body(*arguments)
+    vocab_rows = arguments[2].shape[0]
+    return lax.cond(
+        most <= SLOTS,
+        lambda *given: place(given[0], given[1], vocab_rows),
+        lambda *given: dense_body(*given[2:]),
+        lid_row,
+        sums,
+        *arguments,
+    )
+
+
 def solution(mesh):
     return jax.shard_map(
         body,

time: 1360 us -> 205 us (0.15)
  waiting for transfers between devices: 1070 us -> 0 us
  Pallas kernels: 0 us -> 187 us
  other arithmetic: 138 us -> 0.02 us
  matrix products: 59.6 us -> 0 us
  starting transfers between devices: 46.5 us -> 0 us
  local copies, waits for them, and re-layouts: 27.6 us -> 3.51 us
    psum x10 -> x0, waiting for transfers between devices: 742 us -> none  [narrow(): return lax.psum(terms.astype(jnp.bfloat16), 'mp').astype(jnp.float32)]
    pallas_call x0 -> x4, Pallas kernels: none -> 187 us  [the longest x1 85.5 us: fast_body(): pl.pallas_call(functools.partial(gather_kernel, sections, replicas, parts...]
    all_gather x4 -> x0, waiting for transfers between devices: 150 us -> none  [the longest x1 99.1 us: body(): lax.all_gather(own_cols.reshape(-1, piece_width), ('section', 'dp'), axis...]
    reduce_scatter x1 -> x0, waiting for transfers between devices: 140 us -> none  [body(): lax.psum_scatter(picked.astype(jnp.float32).astype(jnp.bfloat16), ('secti...]
    dot_general x30 -> x0, matrix products: 59.6 us -> none  [the longest x5 18.2 us: forward_block(): jnp.dot(hidden, down_weight, preferred_element_type=jnp.float32)]
    reduce_sum x35 -> x0, other arithmetic: 48.3 us -> none  [the longest x25 31.2 us: inverse_rms(): return lax.rsqrt(jnp.mean(values * values, axis=-1, keepdims=True) + EPS)]
    ppermute x10 -> x0, starting transfers between devices: 46.2 us -> none  [from_behind(): lax.ppermute(value, axis, [(source, source + steps) for source in range(f...]
    scatter-add x1 -> x0, other arithmetic: 39.7 us -> none  [body(): table = jax.ops.segment_sum(masked, safe_ids, num_segments=vocab_rows)]
  transfers between devices with their start and end apart: 25 -> 0, of which waited for: 18 -> 0; matrix products, arithmetic and copies ran while one was open for 1% -> 0% of each run, Pallas kernels for 0% -> 0%
where the time goes in v1:
time: 205 us; the launch traced here: 204 us
  Pallas kernels  187 us (91%)
  between operations  14.2 us (7%)
  local copies, waits for them, and re-layouts  3.51 us (2%)
    pallas_call x1, Pallas kernels, fast_body(): pl.pallas_call(functools.partial(gather_kernel, sections, replicas, parts...  85.5 us
    pallas_call x1, Pallas kernels, fast_body(): pl.pallas_call(functools.partial(scatter_kernel, sections, replicas), out...  48.2 us
    pallas_call x1, Pallas kernels, fast_body(): pl.pallas_call(functools.partial(block_kernel, parts), out_shape=jax.Shap...  46.3 us
    pallas_call x1, Pallas kernels, place(): pl.pallas_call(place_kernel, grid=(vocab_rows // block,), out_shape=jax.S...  6.48 us

profile of v1, /device:TPU:1, one launch (start us, length us, event | category | flops | bytes accessed | tf_op | source)
XLA Modules:
  0.0 204.4 jit_solution(11312677811849103384)
XLA Ops:
  6.5 0.8 stack.9
  7.3 0.8 stack.10
  8.2 0.7 reshape.276.ids_ref
  8.9 0.0 copy-start.3
  8.9 0.0 copy-start.4
  8.9 0.0 copy-start.5
  8.9 0.0 copy-start.7
  8.9 85.5 %gather_rows.1 = (bf16[128,896]{1,0:T(8,128)(2,1)}, s32[8,128]{1,0:T(8,128)}, s32[8,512]{1,0:T(8,128)S(1)}, f32[8,128]{1,0:T(8,128)}, bf16[8,896,256]{2,1,0:T(8,128)(2,1)}, /*index=5*/bf16[8,128,896]{2,1,0:T(8,128)(2,1)}) custom-call(s32[32,128]{1,0:T(8,128)} %reshape.276.ids_ref, bf16[2048,896]{1,0:T(8,128)(2,1)} %table_hbm.1, bf16[7168,128]{1,0:T(8,128)(2,1)} %bitcast.121, ...), custom_call_target="tpu_custom_call" | custom-call | tf_op jit(solution)/shard_map/gather_rows/pallas_call | solution.py:817
  94.4 0.0 copy-done.3
  94.4 0.0 copy-done.4
  94.4 0.0 copy-done.5
  94.4 0.0 copy-done.7
  94.4 0.0 copy-start
  94.4 0.0 copy-start.9
  94.4 0.0 copy-start.10
  94.5 46.3 %blocks.1.grad_ref = bf16[128,896]{1,0:T(8,128)(2,1)} custom-call(bf16[128,896]{1,0:T(8,128)(2,1)} %get-tuple-element.592.rows_ref, bf16[128,896]{1,0:T(8,128)(2,1)S(1)} %bitcast.144, bf16[128,896]{1,0:T(8,128)(2,1)S(1)} %bitcast.143, bf16[8,896,256]{2,1,0:T(8,128)(2,1)} %get-tuple-element.593.gu_ref, bf16[8,128,896]{2,1,0:T(8,128)(2,1)} %get-tuple-element.594.down_ref, ...), custom_call_target="tpu_custom_call" | custom-call | tf_op jit(solution)/shard_map/blocks/pallas_call | solution.py:848
  140.8 48.2 %scatter_rows.1 = bf16[32,16,896]{2,1,0:T(8,128)(2,1)} custom-call(bf16[128,896]{1,0:T(8,128)(2,1)} %blocks.1.grad_ref, s32[8,128]{1,0:T(8,128)} %get-tuple-element.595.slot_ref), custom_call_target="tpu_custom_call" | custom-call | tf_op jit(solution)/shard_map/scatter_rows/pallas_call | solution.py:890
  189.0 1.2 slice.86
  190.8 0.0 copy-done
  190.9 0.0 copy-done.9
  190.9 0.0 copy-done.10
  190.9 6.7 %conditional.1 = (bf16[2048,896]{1,0:T(8,128)(2,1)}) conditional(s32[]{:T(128)} %bitcast.29, (s32[4,512]{1,0:T(4,128)S(1)}, s32[4,512]{1,0:T(4,128)S(1)}, bf16[2048,896]{1,0:T(8,128)(2,1)}, bf16[1,7168,128]{2,1,0:T(8,128)(2,1)S(1)}, bf16[1,7168,128]{2,1,0:T(8,128)(2,1)}, /*index=5*/bf16[1,128,7168]{2,1,0:T(8,128)(2,1)}, f32[2,7168]{1,0:T(2,128)S(1)}, ...), branch_computations={%region_0.18_spmd, %region_18.19_spmd} | conditional | flops 514539904 | bytes 182974272 | solution.py:926
  191.1 6.5 %place_rows.1 = bf16[2048,896]{1,0:T(8,128)(2,1)} custom-call(s32[8,512]{1,0:T(8,128)S(1)} %get-tuple-element.583.lid_ref, bf16[512,896]{1,0:T(8,128)(2,1)} %bitcast.139), custom_call_target="tpu_custom_call" | custom-call | tf_op jit(solution)/shard_map/cond/branch_1_fun/place_rows/pallas_call | solution.py:910
  (3 shorter events, 0.1 us)
Async XLA Ops:
  8.9 85.5 %copy-start.3 = (f32[1,7168]{1,0:T(1,128)S(1)}, f32[1,7168]{1,0:T(1,128)}, u32[]{:S(2)}) copy-start(f32[1,7168]{1,0:T(1,128)} %gain_ref.1) | copy-start | bytes 86020
  8.9 85.5 %copy-start.4 = (f32[2,7168]{1,0:T(2,128)S(1)}, f32[2,7168]{1,0:T(2,128)}, u32[]{:S(2)}) copy-start(f32[2,7168]{1,0:T(2,128)} %mtp_gain_ref.1) | copy-start | bytes 172036
  8.9 85.5 %copy-start.5 = (bf16[4,32,896]{2,1,0:T(8,128)(2,1)S(1)}, bf16[4,32,896]{2,1,0:T(8,128)(2,1)}, u32[]{:S(2)}) copy-start(bf16[4,32,896]{2,1,0:T(8,128)(2,1)} %param.29) | copy-start | bytes 688132
  8.9 85.5 %copy-start.7 = (bf16[4,32,896]{2,1,0:T(8,128)(2,1)S(1)}, bf16[4,32,896]{2,1,0:T(8,128)(2,1)}, u32[]{:S(2)}) copy-start(bf16[4,32,896]{2,1,0:T(8,128)(2,1)} %param.28) | copy-start | bytes 688132
  94.4 96.4 %copy-start = (bf16[1,7168,128]{2,1,0:T(8,128)(2,1)S(1)}, bf16[1,7168,128]{2,1,0:T(8,128)(2,1)}, u32[]{:S(2)}) copy-start(bf16[1,7168,128]{2,1,0:T(8,128)(2,1)} %param.24) | copy-start | bytes 5505028
  94.4 96.4 %copy-start.9 = (s32[4,512]{1,0:T(4,128)S(1)}, s32[4,512]{1,0:T(4,128)}, u32[]{:S(2)}) copy-start(s32[4,512]{1,0:T(4,128)} %param.21) | copy-start | bytes 24580
  94.4 96.4 %copy-start.10 = (s32[4,512]{1,0:T(4,128)S(1)}, s32[4,512]{1,0:T(4,128)}, u32[]{:S(2)}) copy-start(s32[4,512]{1,0:T(4,128)} %param.20) | copy-start | bytes 24580

commit v2 on v0

--- a/solution.py
+++ b/solution.py
@@ -1,6 +1,10 @@
+import functools
+
 import jax
 import jax.numpy as jnp
 from jax import lax
+from jax.experimental import pallas as pl
+from jax.experimental.pallas import tpu as pltpu
 from jax.sharding import PartitionSpec as P
 
 EPS = 1e-06
@@ -79,7 +83,7 @@
     return grad_out.astype(jnp.float32) + norm_back(stream.astype(jnp.float32), gain * grad_normed)
 
 
-def body(
+def dense_body(
     token_ids, next_ids, embed_table, norm_gain, w_gate, w_up, w_down, mtp_gain, main_cot, mtp_cot
 ):
     sections = lax.axis_size("section")
@@ -175,6 +179,805 @@
     return table.astype(jnp.bfloat16)
 
 
+MESH = pl.DeviceIdType.MESH
+SLOTS = 16
+BF = jnp.bfloat16
+F32 = jnp.float32
+COLS = (((1,), (1,)), ((), ()))
+
+
+def dot(a, b):
+    return jnp.dot(a, b, preferred_element_type=F32)
+
+
+def dot_t(a, b):
+    return lax.dot_general(a, b, COLS, preferred_element_type=F32)
+
+
+def iota(shape, axis):
+    return lax.broadcasted_iota(jnp.int32, shape, axis)
+
+
+def loop(count, one):
+    def step(index, carry):
+        one(index)
+        return carry
+
+    lax.fori_loop(0, count, step, 0)
+
+
+def remote(source, target, send_sem, recv_sem, device):
+    return pltpu.make_async_remote_copy(
+        src_ref=source,
+        dst_ref=target,
+        send_sem=send_sem,
+        recv_sem=recv_sem,
+        device_id=device,
+        device_id_type=MESH,
+    )
+
+
+def to_column(row):
+    count = row.shape[1]
+    eye = iota((count, count), 0) == iota((count, count), 1)
+    whole = jnp.broadcast_to(row, (count, count))
+    return jnp.sum(jnp.where(eye, whole, jnp.zeros_like(whole)), axis=1, keepdims=True)
+
+
+def to_row(column):
+    count = column.shape[0]
+    eye = iota((count, count), 0) == iota((count, count), 1)
+    whole = jnp.broadcast_to(column, (count, count))
+    return jnp.sum(jnp.where(eye, whole, jnp.zeros_like(whole)), axis=0, keepdims=True)
+
+
+def total(values):
+    return jnp.sum(values, axis=1, keepdims=True)
+
+
+def step_kernel(
+    sections,
+    replicas,
+    parts,
+    ids_ref,
+    main_cot_ref,
+    mtp_cot_ref,
+    gain_ref,
+    mtp_gain_ref,
+    table_hbm,
+    gate_hbm,
+    up_hbm,
+    down_hbm,
+    sums_ref,
+    lid_ref,
+    over_ref,
+    table,
+    first,
+    rank,
+    lid,
+    onehot,
+    send,
+    recv,
+    rows_ref,
+    grad_ref,
+    gu,
+    down,
+    relay_gu,
+    relay_down,
+    part_out,
+    part_in,
+    early_out,
+    early_in,
+    narrow_in,
+    wide_in,
+    stat_in,
+    cross,
+    hold,
+    table_sem,
+    local_sem,
+    row_send,
+    row_recv,
+    sum_send,
+    sum_recv,
+    weight_local,
+    weight_send,
+    weight_recv,
+    relay_send,
+    relay_recv,
+    part_send,
+    part_recv,
+    early_send,
+    early_recv,
+    wide_send,
+    wide_recv,
+    narrow_send,
+    narrow_recv,
+    stat_send,
+    stat_recv,
+    cross_send,
+    cross_recv,
+):
+    section = lax.axis_index("section")
+    replica = lax.axis_index("dp")
+    part = lax.axis_index("mp")
+    count = sections * replicas
+    me = section * replicas + replica
+    vocab_rows, width = table_hbm.shape
+    hidden = gate_hbm.shape[1]
+    tokens = ids_ref.shape[1]
+    model_width = parts * width
+    slots = count * SLOTS
+    ring = parts // 2
+    load = pltpu.make_async_copy(table_hbm, table, table_sem)
+    load.start()
+
+    def column_peer(step):
+        there = step // replicas
+        other = lax.rem(replica + 1 + step, replicas)
+        return there * replicas + other, (there, other, part)
+
+    def away(ahead, across):
+        return lax.rem(part // 2 + ahead, ring) * 2 + lax.rem(part + across, 2)
+
+    def row_peer(step):
+        ahead = jnp.where(
+            step < 2,
+            1 + step * (ring - 2),
+            jnp.where(step == 2, 0, jnp.where(step < 5, 1 + (step - 3) * (ring - 2), 2)),
+        )
+        across = jnp.where(step < 2, 0, jnp.where(step < 5, 1, step - 5))
+        other = away(ahead, across)
+        return other, (section, replica, other)
+
+    barrier = pltpu.get_barrier_semaphore()
+
+    def greet_column(step):
+        other, device = column_peer(step)
+
+        @pl.when(other != me)
+        def _():
+            pl.semaphore_signal(barrier, inc=1, device_id=device, device_id_type=MESH)
+
+    def greet_row(step):
+        other = lax.rem(part + 1 + lax.rem(step, parts - 1), parts)
+        there = jnp.where(step < parts - 1, section, 1 - section)
+        pl.semaphore_signal(
+            barrier, inc=1, device_id=(there, replica, other), device_id_type=MESH
+        )
+
+    loop(count, greet_column)
+    loop(2 * (parts - 1), greet_row)
+    pl.semaphore_wait(barrier, count - 1 + 2 * (parts - 1))
+
+    def weight_source(target):
+        features = pl.ds(pl.multiple_of(target * width, width), width)
+        return gate_hbm.at[features, :], up_hbm.at[features, :], down_hbm.at[:, features]
+
+    def weight_slot(origin):
+        return (
+            gu.at[:, pl.ds(pl.multiple_of(origin * 2 * hidden, hidden), hidden)],
+            gu.at[:, pl.ds(pl.multiple_of(origin * 2 * hidden + hidden, hidden), hidden)],
+            down.at[pl.ds(pl.multiple_of(origin * hidden, hidden), hidden), :],
+        )
+
+    def relay_slot(way):
+        return (
+            relay_gu.at[way, :, pl.ds(0, hidden)],
+            relay_gu.at[way, :, pl.ds(hidden, hidden)],
+            relay_down.at[way],
+        )
+
+    def direct_copy(kind, step):
+        other, device = row_peer(step)
+        return remote(
+            weight_source(other)[kind],
+            weight_slot(part)[kind],
+            weight_send.at[kind, step],
+            weight_recv.at[kind, part],
+            device,
+        )
+
+    def relay_copy(kind, way):
+        final = away(2, way)
+        return remote(
+            weight_source(final)[kind],
+            relay_slot(way)[kind],
+            weight_send.at[kind, parts - 3 + way],
+            relay_recv.at[kind, way],
+            (section, replica, away(1 + way * (ring - 2), 0)),
+        )
+
+    def forward_copy(kind, way):
+        origin = away(ring - 1 - way * (ring - 2), 0)
+        final = away(1 + way * (ring - 2), way)
+        return remote(
+            relay_slot(way)[kind],
+            weight_slot(origin)[kind],
+            relay_send.at[kind, way],
+            weight_recv.at[kind, origin],
+            (section, replica, final),
+        )
+
+    def own_weight(kind):
+        return pltpu.make_async_copy(
+            weight_source(part)[kind], weight_slot(part)[kind], weight_local.at[kind]
+        )
+
+    def weights_start():
+        for kind in range(3):
+            for way in range(2):
+                relay_copy(kind, way).start()
+            loop(parts - 3, lambda step: direct_copy(kind, step).start())
+        for kind in range(3):
+            own_weight(kind).start()
+
+    def relay_on(kinds):
+        for kind in kinds:
+            for way in range(2):
+                relay_copy(kind, way).wait_recv()
+                forward_copy(kind, way).start()
+
+    def weight_wait(kind, step):
+        other, device = row_peer(step)
+        remote(
+            weight_slot(other)[kind],
+            weight_slot(other)[kind],
+            weight_send.at[kind, step],
+            weight_recv.at[kind, other],
+            device,
+        ).wait_recv()
+
+    @pl.when(section == 0)
+    def _():
+        weights_start()
+
+    earlier = iota((tokens, tokens), 0) < iota((tokens, tokens), 1)
+
+    def find_first(step):
+        for inner in range(4):
+            index = pl.ds(step * 4 + inner, 1)
+            row = ids_ref[index, :]
+            same = (to_column(row) == row) & earlier
+            seen = jnp.max(jnp.where(same, 1.0, 0.0), axis=0, keepdims=True)
+            first[index, :] = 1.0 - seen
+
+    loop(count // 4, find_first)
+    shard = ids_ref[...] // vocab_rows
+    mine = jnp.where(shard == me, first[...], 0.0)
+    triangle = jnp.where(earlier, 1.0, 0.0).astype(BF)
+    rank[...] = jnp.where(mine > 0.0, dot(mine.astype(BF), triangle), -1.0)
+
+    def find_lid(step):
+        for inner in range(4):
+            index = step * 4 + inner
+            row = ids_ref[pl.ds(index, 1), :] - me * vocab_rows + 1
+            picks = rank[pl.ds(index, 1), :].astype(jnp.int32) == iota((SLOTS, tokens), 0)
+            found = jnp.sum(
+                jnp.where(picks, jnp.broadcast_to(row, picks.shape), 0), axis=1, keepdims=True
+            )
+            lid[pl.ds(pl.multiple_of(index * SLOTS, SLOTS), SLOTS), :] = jnp.broadcast_to(
+                found - 1, (SLOTS, tokens)
+            )
+
+    loop(count // 4, find_lid)
+    load.wait()
+
+    def row_copy(step):
+        other, device = column_peer(step)
+        return remote(send.at[other], recv.at[me], row_send.at[step], row_recv.at[me], device)
+
+    for half in range(sections):
+
+        def mark(step):
+            other = column_peer(half * replicas + step)[0]
+            wanted = lid[pl.ds(pl.multiple_of(other * SLOTS, SLOTS), SLOTS), :]
+            place = pl.ds(pl.multiple_of(step * SLOTS, SLOTS), SLOTS)
+            for lane in range(vocab_rows // tokens):
+                hit = wanted == iota(wanted.shape, 1) + lane * tokens
+                onehot[place, pl.ds(lane * tokens, tokens)] = jnp.where(hit, 1.0, 0.0).astype(BF)
+
+        loop(replicas, mark)
+        found = dot(onehot[...], table[...]).astype(BF)
+        for step in range(replicas):
+            here = half * replicas + step
+            other = column_peer(here)[0]
+            send[other] = found[step * SLOTS : (step + 1) * SLOTS]
+
+        def go(step):
+            here = half * replicas + step
+
+            @pl.when(column_peer(here)[0] != me)
+            def _():
+                row_copy(here).start()
+
+        loop(replicas, go)
+    recv[me] = send[me]
+
+    @pl.when(section == 1)
+    def _():
+        weights_start()
+
+    relay_on((0, 1))
+
+    def fill(index, most):
+        held = jnp.where(shard == index, first[...], 0.0)
+        return jnp.maximum(most, total(held))
+
+    most = lax.fori_loop(0, count, fill, jnp.zeros((count, 1), F32))
+    over_ref[...] = jnp.broadcast_to(jnp.max(most, axis=0, keepdims=True), over_ref.shape)
+    eye = iota((tokens, tokens), 0) == iota((tokens, tokens), 1)
+    for block in range(slots // tokens):
+        rows = pl.ds(block * tokens, tokens)
+        row = jnp.sum(jnp.where(eye, lid[rows, :], 0), axis=0, keepdims=True)
+        lid_ref[:, rows] = jnp.broadcast_to(row, (8, tokens))
+    own_row = ids_ref[pl.ds(me, 1), :]
+    own_first = first[pl.ds(me, 1), :]
+    own_column = to_column(own_row)
+    shard_row = own_row // vocab_rows
+    counted = (own_column // vocab_rows == shard_row) & earlier & (to_column(own_first) > 0.0)
+    slot_row = shard_row * SLOTS + jnp.sum(jnp.where(counted, 1, 0), axis=0, keepdims=True)
+    leads = (own_column == own_row) & (own_first > 0.0)
+    slot_column = total(jnp.where(leads, jnp.broadcast_to(slot_row, leads.shape), 0))
+
+    def row_wait(step):
+        other, device = column_peer(step)
+
+        @pl.when(other != me)
+        def _():
+            remote(
+                send.at[me], recv.at[other], row_send.at[step], row_recv.at[other], device
+            ).wait_recv()
+
+    loop(count, row_wait)
+    spread = jnp.where(slot_column == iota((tokens, slots), 1), 1.0, 0.0).astype(BF)
+    rows_ref[...] = dot(spread, recv[...].reshape(slots, width)).astype(BF)
+
+    features = pl.ds(pl.multiple_of(part * width, width), width)
+    gain = gain_ref[0:1, features]
+    gain_main = mtp_gain_ref[0:1, features]
+    gain_next = mtp_gain_ref[1:2, features]
+
+    def inverse(sum_of_squares):
+        return lax.rsqrt(sum_of_squares / model_width + EPS)
+
+    def lanes(index, size):
+        return pl.ds(pl.multiple_of(index * size, size), size)
+
+    def put_stats(slot, columns):
+        rows = [to_row(column) for column in columns]
+        rows = rows + [jnp.zeros_like(rows[0])] * (8 - len(rows))
+        stat_in[slot, part] = jnp.concatenate(rows, axis=0)
+
+    def get_stats(slot, number):
+        value = stat_in[slot, 0]
+        for index in range(1, parts):
+            value = value + stat_in[slot, index]
+        return [to_column(value[index : index + 1, :]) for index in range(number)]
+
+    def stat_copy(slot, step):
+        return remote(
+            stat_in.at[slot, part],
+            stat_in.at[slot, part],
+            stat_send.at[slot, step],
+            stat_recv.at[slot, part],
+            row_peer(step)[1],
+        )
+
+    def share_stats(slot):
+        loop(parts - 1, lambda step: stat_copy(slot, step).start())
+
+    def wait_stats(slot):
+        def one(step):
+            other, device = row_peer(step)
+            remote(
+                stat_in.at[slot, other],
+                stat_in.at[slot, other],
+                stat_send.at[slot, step],
+                stat_recv.at[slot, other],
+                device,
+            ).wait()
+
+        loop(parts - 1, one)
+
+    def tell_copy(step):
+        other = lax.rem(part + step, parts)
+        return remote(
+            stat_in.at[1, part],
+            stat_in.at[1, part],
+            stat_send.at[1, step],
+            stat_recv.at[1, part],
+            (1 - section, replica, other),
+        )
+
+    def gate_up_start(normed):
+        def partial(other):
+            part_out[other] = dot(normed, gu[:, lanes(other, 2 * hidden)]).astype(BF)
+
+        def one(step):
+            other, device = row_peer(step)
+            weight_wait(0, step)
+            weight_wait(1, step)
+            partial(other)
+            remote(
+                part_out.at[other],
+                part_in.at[part],
+                part_send.at[step],
+                part_recv.at[part],
+                device,
+            ).start()
+
+        loop(parts - 1, one)
+        own_weight(0).wait()
+        own_weight(1).wait()
+        partial(part)
+
+    def gate_up_wait():
+        def one(step, value):
+            other, device = row_peer(step)
+            remote(
+                part_in.at[other],
+                part_in.at[other],
+                part_send.at[step],
+                part_recv.at[other],
+                device,
+            ).wait()
+            return value + part_in[other].astype(F32)
+
+        return lax.fori_loop(0, parts - 1, one, part_out[part].astype(F32))
+
+    def down_wait():
+        loop(parts - 1, lambda step: weight_wait(2, step))
+        own_weight(2).wait()
+
+    def grad_hidden_start(grad):
+        early_out[...] = dot_t(grad, down[...]).astype(BF)
+
+        def one(step):
+            other, device = row_peer(step)
+            remote(
+                early_out.at[:, lanes(other, hidden)],
+                early_in.at[part],
+                early_send.at[step],
+                early_recv.at[part],
+                device,
+            ).start()
+
+        loop(parts - 1, one)
+
+    def grad_hidden_wait():
+        def one(step, value):
+            other, device = row_peer(step)
+            remote(
+                early_in.at[other],
+                early_in.at[other],
+                early_send.at[step],
+                early_recv.at[other],
+                device,
+            ).wait()
+            return value + early_in[other].astype(F32)
+
+        return lax.fori_loop(
+            0, parts - 1, one, early_out[:, lanes(part, hidden)].astype(F32)
+        )
+
+    def share_columns(whole, size, send_sem, recv_sem):
+        def start(step):
+            device = row_peer(step)[1]
+            own = whole.at[:, lanes(part, size)]
+            remote(own, own, send_sem.at[step], recv_sem.at[part], device).start()
+
+        def wait(step):
+            other, device = row_peer(step)
+            theirs = whole.at[:, lanes(other, size)]
+            remote(theirs, theirs, send_sem.at[step], recv_sem.at[other], device).wait()
+
+        loop(parts - 1, start)
+        loop(parts - 1, wait)
+
+    def backward(gate, up, grad_hidden):
+        sigmoid = jax.nn.sigmoid(gate)
+        grad_gate = grad_hidden * up * sigmoid * (1.0 + gate * (1.0 - sigmoid))
+        grad_up = grad_hidden * gate * sigmoid
+        wide_in[:, lanes(part, 2 * hidden)] = jnp.concatenate(
+            [grad_gate, grad_up], axis=1
+        ).astype(BF)
+        share_columns(wide_in, 2 * hidden, wide_send, wide_recv)
+        return dot_t(wide_in[...], gu[...]) * gain
+
+    over = remote(
+        cross.at[0], cross.at[1], cross_send, cross_recv, (1 - section, replica, part)
+    )
+
+    @pl.when(section == 0)
+    def _():
+        rows = rows_ref[...].astype(F32)
+        put_stats(0, [total(rows * rows)])
+        share_stats(0)
+        gate_up_start((rows * gain).astype(BF))
+        relay_on((2,))
+        wait_stats(0)
+        scale = inverse(get_stats(0, 1)[0])
+        whole = gate_up_wait() * scale
+        hold[...] = whole
+        gate = whole[:, :hidden]
+        up = whole[:, hidden:]
+        narrow_in[:, lanes(part, hidden)] = (gate * jax.nn.sigmoid(gate) * up).astype(BF)
+        share_columns(narrow_in, hidden, narrow_send, narrow_recv)
+        down_wait()
+        out = rows_ref[...].astype(F32) + dot(narrow_in[...], down[...])
+        cross[0] = out.astype(BF)
+        over.start()
+        main = cross[0].astype(F32)
+        put_stats(1, [total(main * main)])
+        loop(parts, lambda step: tell_copy(step).start())
+        loop(parts, lambda step: tell_copy(step).wait_send())
+        over.wait()
+        grad = cross[1]
+        grad_hidden_start(grad)
+        grad_hidden = grad_hidden_wait()
+        whole = hold[...]
+        scaled = backward(whole[:, :hidden], whole[:, hidden:], grad_hidden)
+        rows = rows_ref[...].astype(F32)
+        put_stats(2, [total(rows * scaled)])
+        share_stats(2)
+        wait_stats(2)
+        mean = get_stats(2, 1)[0] / model_width
+        scale = inverse(get_stats(0, 1)[0])
+        result = grad.astype(F32) + scale * scaled - rows * (scale * scale * scale * mean)
+        grad_ref[...] = result.astype(BF)
+
+    @pl.when(section == 1)
+    def _():
+        rows = rows_ref[...].astype(F32)
+        put_stats(0, [total(rows * rows)])
+        share_stats(0)
+        relay_on((2,))
+        wait_stats(0)
+        scale_next = inverse(get_stats(0, 1)[0])
+        down_wait()
+        grad_hidden_start(mtp_cot_ref[...])
+        grad_hidden = grad_hidden_wait()
+
+        def heard(index):
+            remote(
+                stat_in.at[1, index],
+                stat_in.at[1, index],
+                stat_send.at[1, 0],
+                stat_recv.at[1, index],
+                (1 - section, replica, part),
+            ).wait_recv()
+
+        loop(parts, heard)
+        over.wait_recv()
+        scale_main = inverse(get_stats(1, 1)[0])
+        main = cross[1].astype(F32)
+        mixed = (main * scale_main * gain_main + rows * scale_next * gain_next).astype(BF)
+        mixed = mixed.astype(F32)
+        put_stats(2, [total(mixed * mixed)])
+        share_stats(2)
+        gate_up_start((mixed * gain).astype(BF))
+        wait_stats(2)
+        scale = inverse(get_stats(2, 1)[0])
+        whole = gate_up_wait() * scale
+        scaled = backward(whole[:, :hidden], whole[:, hidden:], grad_hidden)
+        cot = mtp_cot_ref[...].astype(F32)
+        next_weighted = rows * gain_next
+        main_weighted = main * gain_main
+        put_stats(
+            3,
+            [
+                total(mixed * scaled),
+                total(next_weighted * scaled),
+                total(next_weighted * mixed),
+                total(next_weighted * cot),
+                total(main_weighted * scaled),
+                total(main_weighted * mixed),
+                total(main_weighted * cot),
+            ],
+        )
+        share_stats(3)
+        wait_stats(3)
+        s1, s2, s3, s4, s5, s6, s7 = get_stats(3, 7)
+        slope = scale * scale * scale * (s1 / model_width)
+        grad_mixed = cot + scale * scaled - mixed * slope
+        mean_next = (s4 + scale * s2 - slope * s3) / model_width
+        mean_main = (s7 + scale * s5 - slope * s6) / model_width
+        grad_main = (
+            main_cot_ref[...].astype(F32)
+            + scale_main * (gain_main * grad_mixed)
+            - main * (scale_main * scale_main * scale_main * mean_main)
+        )
+        cross[0] = grad_main.astype(BF)
+        over.start()
+        grad_next = scale_next * (gain_next * grad_mixed) - rows * (
+            scale_next * scale_next * scale_next * mean_next
+        )
+        grad_ref[...] = grad_next.astype(BF)
+        over.wait_send()
+
+    def row_done(step):
+        @pl.when(column_peer(step)[0] != me)
+        def _():
+            row_copy(step).wait_send()
+
+    loop(count, row_done)
+    back = jnp.where(to_row(slot_column) == iota((slots, tokens), 0), 1.0, 0.0).astype(BF)
+    send[...] = dot(back, grad_ref[...]).astype(BF).reshape(count, SLOTS, width)
+
+    def sum_copy(step):
+        other, device = column_peer(step)
+        return remote(
+            send.at[other], sums_ref.at[me], sum_send.at[step], sum_recv.at[me], device
+        )
+
+    def sum_start(step):
+        @pl.when(column_peer(step)[0] != me)
+        def _():
+            sum_copy(step).start()
+
+    loop(count, sum_start)
+    sums_ref[me] = send[me]
+
+    for kind in range(3):
+        for way in range(2):
+            relay_copy(kind, way).wait_send()
+            forward_copy(kind, way).wait_send()
+        loop(parts - 3, lambda step: direct_copy(kind, step).wait_send())
+
+    def sum_wait(step):
+        other, device = column_peer(step)
+
+        @pl.when(other != me)
+        def _():
+            remote(
+                send.at[other],
+                sums_ref.at[other],
+                sum_send.at[step],
+                sum_recv.at[other],
+                device,
+            ).wait()
+
+    loop(count, sum_wait)
+
+
+def place_kernel(lid_ref, sums_ref, out_ref):
+    rows = out_ref.shape[0]
+    slots = sums_ref.shape[0]
+    base = pl.program_id(0) * rows
+    hit = lid_ref[0:1, :] == iota((rows, slots), 0) + base
+    out_ref[...] = dot(jnp.where(hit, 1.0, 0.0).astype(BF), sums_ref[...]).astype(BF)
+
+
+def vmem():
+    return pl.BlockSpec(memory_space=pltpu.VMEM)
+
+
+def anywhere():
+    return pl.BlockSpec(memory_space=pl.ANY)
+
+
+def dma(*shape):
+    return pltpu.SemaphoreType.DMA(shape)
+
+
+def fast_body(
+    token_ids, next_ids, embed_table, norm_gain, w_gate, w_up, w_down, mtp_gain, main_cot, mtp_cot
+):
+    sections = lax.axis_size("section")
+    replicas = lax.axis_size("dp")
+    parts = lax.axis_size("mp")
+    count = sections * replicas
+    batches = token_ids.shape[0]
+    row_count = token_ids.shape[1] // replicas
+    tokens = batches * row_count
+    vocab_rows, width = embed_table.shape
+    hidden = w_gate.shape[2]
+    ids = jnp.stack([token_ids, next_ids]).reshape(sections, batches, replicas, row_count)
+    ids = ids.transpose(0, 2, 1, 3).reshape(count, tokens)
+    slots = count * SLOTS
+    sums, lid_row, most = pl.pallas_call(
+        functools.partial(step_kernel, sections, replicas, parts),
+        out_shape=(
+            jax.ShapeDtypeStruct((count, SLOTS, width), BF),
+            jax.ShapeDtypeStruct((8, slots), jnp.int32),
+            jax.ShapeDtypeStruct((8, 128), F32),
+        ),
+        in_specs=[vmem()] * 5 + [anywhere()] * 4,
+        out_specs=(vmem(), vmem(), vmem()),
+        scratch_shapes=[
+            pltpu.VMEM((vocab_rows, width), BF),
+            pltpu.VMEM((count, tokens), F32),
+            pltpu.VMEM((count, tokens), F32),
+            pltpu.VMEM((slots, tokens), jnp.int32),
+            pltpu.VMEM((replicas * SLOTS, vocab_rows), BF),
+            pltpu.VMEM((count, SLOTS, width), BF),
+            pltpu.VMEM((count, SLOTS, width), BF),
+            pltpu.VMEM((tokens, width), BF),
+            pltpu.VMEM((tokens, width), BF),
+            pltpu.VMEM((width, parts * 2 * hidden), BF),
+            pltpu.VMEM((parts * hidden, width), BF),
+            pltpu.VMEM((2, width, 2 * hidden), BF),
+            pltpu.VMEM((2, hidden, width), BF),
+            pltpu.VMEM((parts, tokens, 2 * hidden), BF),
+            pltpu.VMEM((parts, tokens, 2 * hidden), BF),
+            pltpu.VMEM((tokens, parts * hidden), BF),
+            pltpu.VMEM((parts, tokens, hidden), BF),
+            pltpu.VMEM((tokens, parts * hidden), BF),
+            pltpu.VMEM((tokens, parts * 2 * hidden), BF),
+            pltpu.VMEM((4, parts, 8, tokens), F32),
+            pltpu.VMEM((2, tokens, width), BF),
+            pltpu.VMEM((tokens, 2 * hidden), F32),
+            pltpu.SemaphoreType.DMA,
+            pltpu.SemaphoreType.DMA,
+            dma(count),
+            dma(count),
+            dma(count),
+            dma(count),
+            dma(3),
+            dma(3, parts),
+            dma(3, parts),
+            dma(3, 2),
+            dma(3, 2),
+            dma(parts),
+            dma(parts),
+            dma(parts),
+            dma(parts),
+            dma(parts),
+            dma(parts),
+            dma(parts),
+            dma(parts),
+            dma(4, parts),
+            dma(4, parts),
+            pltpu.SemaphoreType.DMA,
+            pltpu.SemaphoreType.DMA,
+        ],
+        compiler_params=pltpu.CompilerParams(
+            collective_id=0, has_side_effects=True, vmem_limit_bytes=56 << 20
+        ),
+        name="train_step",
+    )(
+        ids,
+        main_cot.reshape(tokens, width),
+        mtp_cot.reshape(tokens, width),
+        norm_gain,
+        mtp_gain,
+        embed_table,
+        w_gate[0],
+        w_up[0],
+        w_down[0],
+    )
+    return most[0, 0], lid_row, sums.reshape(slots, width)
+
+
+def place(lid_row, sums, vocab_rows):
+    slots, width = sums.shape
+    block = vocab_rows // 8
+    return pl.pallas_call(
+        place_kernel,
+        grid=(vocab_rows // block,),
+        out_shape=jax.ShapeDtypeStruct((vocab_rows, width), BF),
+        in_specs=[
+            pl.BlockSpec((8, slots), lambda i: (0, 0)),
+            pl.BlockSpec((slots, width), lambda i: (0, 0)),
+        ],
+        out_specs=pl.BlockSpec((block, width), lambda i: (i, 0)),
+        name="place_rows",
+    )(lid_row, sums)
+
+
+def body(*arguments):
+    most, lid_row, sums = fast_body(*arguments)
+    vocab_rows = arguments[2].shape[0]
+    return lax.cond(
+        most <= SLOTS,
+        lambda *given: place(given[0], given[1], vocab_rows),
+        lambda *given: dense_body(*given[2:]),
+        lid_row,
+        sums,
+        *arguments,
+    )
+
+
 def solution(mesh):
     return jax.shard_map(
         body,

time: 1360 us -> 178 us (0.13)
  waiting for transfers between devices: 1070 us -> 0 us
  Pallas kernels: 0 us -> 160 us
  other arithmetic: 138 us -> 0.02 us
  matrix products: 59.6 us -> 0 us
  starting transfers between devices: 46.5 us -> 0 us
  local copies, waits for them, and re-layouts: 27.6 us -> 3.49 us
    psum x10 -> x0, waiting for transfers between devices: 742 us -> none  [narrow(): return lax.psum(terms.astype(jnp.bfloat16), 'mp').astype(jnp.float32)]
    pallas_call x0 -> x2, Pallas kernels: none -> 160 us  [the longest x1 154 us: fast_body(): pl.pallas_call(functools.partial(step_kernel, sections, replicas, parts),...]
    all_gather x4 -> x0, waiting for transfers between devices: 150 us -> none  [the longest x1 99.1 us: body(): lax.all_gather(own_cols.reshape(-1, piece_width), ('section', 'dp'), axis...]
    reduce_scatter x1 -> x0, waiting for transfers between devices: 140 us -> none  [body(): lax.psum_scatter(picked.astype(jnp.float32).astype(jnp.bfloat16), ('secti...]
    dot_general x30 -> x0, matrix products: 59.6 us -> none  [the longest x5 18.2 us: forward_block(): jnp.dot(hidden, down_weight, preferred_element_type=jnp.float32)]
    reduce_sum x35 -> x0, other arithmetic: 48.3 us -> none  [the longest x25 31.2 us: inverse_rms(): return lax.rsqrt(jnp.mean(values * values, axis=-1, keepdims=True) + EPS)]
    ppermute x10 -> x0, starting transfers between devices: 46.2 us -> none  [from_behind(): lax.ppermute(value, axis, [(source, source + steps) for source in range(f...]
    scatter-add x1 -> x0, other arithmetic: 39.7 us -> none  [body(): table = jax.ops.segment_sum(masked, safe_ids, num_segments=vocab_rows)]
  transfers between devices with their start and end apart: 25 -> 0, of which waited for: 18 -> 0; matrix products, arithmetic and copies ran while one was open for 1% -> 0% of each run, Pallas kernels for 0% -> 0%
where the time goes in v2:
time: 178 us
  Pallas kernels  160 us (90%)
  between operations  14.1 us (8%)
  local copies, waits for them, and re-layouts  3.49 us (2%)
    pallas_call x1, Pallas kernels, fast_body(): pl.pallas_call(functools.partial(step_kernel, sections, replicas, parts),...  154 us
    pallas_call x1, Pallas kernels, place(): pl.pallas_call(place_kernel, grid=(vocab_rows // block,), out_shape=jax.S...  6.48 us

profile of v2, /device:TPU:1, one launch (start us, length us, event | category | flops | bytes accessed | tf_op | source)
XLA Modules:
  0.0 178.1 jit_solution(15475117309837050844)
XLA Ops:
  6.5 0.8 stack.9
  7.3 0.8 stack.10
  8.2 0.7 reshape.276.ids_ref
  8.9 0.0 copy-start
  8.9 0.0 copy-start.3
  8.9 0.0 copy-start.4
  8.9 0.0 copy-start.5
  8.9 0.0 copy-start.6
  8.9 153.7 %train_step.1 = (bf16[32,16,896]{2,1,0:T(8,128)(2,1)}, s32[8,512]{1,0:T(8,128)S(1)}, f32[8,128]{1,0:T(8,128)}) custom-call(s32[32,128]{1,0:T(8,128)} %reshape.276.ids_ref, bf16[128,896]{1,0:T(8,128)(2,1)} %bitcast.142, bf16[128,896]{1,0:T(8,128)(2,1)} %bitcast.143, f32[1,7168]{1,0:T(1,128)} %gain_ref.1, f32[2,7168]{1,0:T(2,128)} %mtp_gain_ref.1, ...), custom_call_target="tpu_custom_call" | custom-call | tf_op jit(solution)/shard_map/train_step/pallas_call | solution.py:878
  162.6 1.2 slice.86
  164.4 0.0 copy-done
  164.5 0.0 copy-done.3
  164.5 0.0 copy-done.4
  164.5 0.0 copy-done.5
  164.5 0.0 copy-done.6
  164.5 6.7 %conditional.1 = (bf16[2048,896]{1,0:T(8,128)(2,1)}) conditional(s32[]{:T(128)} %bitcast.31, (s32[4,512]{1,0:T(4,128)S(1)}, s32[4,512]{1,0:T(4,128)S(1)}, bf16[2048,896]{1,0:T(8,128)(2,1)}, bf16[1,7168,128]{2,1,0:T(8,128)(2,1)S(1)}, bf16[1,7168,128]{2,1,0:T(8,128)(2,1)}, /*index=5*/bf16[1,128,7168]{2,1,0:T(8,128)(2,1)}, f32[2,7168]{1,0:T(2,128)S(1)}, ...), branch_computations={%region_0.18_spmd, %region_18.19_spmd} | conditional | flops 514539904 | bytes 181139200 | solution.py:971
  164.7 6.5 %place_rows.1 = bf16[2048,896]{1,0:T(8,128)(2,1)} custom-call(s32[8,512]{1,0:T(8,128)S(1)} %get-tuple-element.583.lid_ref, bf16[512,896]{1,0:T(8,128)(2,1)} %bitcast.144), custom_call_target="tpu_custom_call" | custom-call | tf_op jit(solution)/shard_map/cond/branch_1_fun/place_rows/pallas_call | solution.py:955
  (3 shorter events, 0.1 us)
Async XLA Ops:
  8.9 155.6 %copy-start = (bf16[1,7168,128]{2,1,0:T(8,128)(2,1)S(1)}, bf16[1,7168,128]{2,1,0:T(8,128)(2,1)}, u32[]{:S(2)}) copy-start(bf16[1,7168,128]{2,1,0:T(8,128)(2,1)} %param.24) | copy-start | bytes 5505028
  8.9 155.6 %copy-start.3 = (f32[1,7168]{1,0:T(1,128)S(1)}, f32[1,7168]{1,0:T(1,128)}, u32[]{:S(2)}) copy-start(f32[1,7168]{1,0:T(1,128)} %gain_ref.1) | copy-start | bytes 86020
  8.9 155.6 %copy-start.4 = (f32[2,7168]{1,0:T(2,128)S(1)}, f32[2,7168]{1,0:T(2,128)}, u32[]{:S(2)}) copy-start(f32[2,7168]{1,0:T(2,128)} %mtp_gain_ref.1) | copy-start | bytes 172036
  8.9 155.6 %copy-start.5 = (s32[4,512]{1,0:T(4,128)S(1)}, s32[4,512]{1,0:T(4,128)}, u32[]{:S(2)}) copy-start(s32[4,512]{1,0:T(4,128)} %param.21) | copy-start | bytes 24580
  8.9 155.6 %copy-start.6 = (s32[4,512]{1,0:T(4,128)S(1)}, s32[4,512]{1,0:T(4,128)}, u32[]{:S(2)}) copy-start(s32[4,512]{1,0:T(4,128)} %param.20) | copy-start | bytes 24580

commit v3 on v2

v3 whole, which is shorter than its diff:
```python
import functools

import jax
import jax.numpy as jnp
from jax import lax
from jax.experimental import pallas as pl
from jax.experimental.pallas import tpu as pltpu
from jax.sharding import PartitionSpec as P

EPS = 1e-06
MESH = pl.DeviceIdType.MESH
FEW_SLOTS = 16
BF = jnp.bfloat16
F32 = jnp.float32
COLS = (((1,), (1,)), ((), ()))


def dot(a, b):
    return jnp.dot(a, b, preferred_element_type=F32)


def dot_t(a, b):
    return lax.dot_general(a, b, COLS, preferred_element_type=F32)


def iota(shape, axis):
    return lax.broadcasted_iota(jnp.int32, shape, axis)


def loop(count, one):
    def step(index, carry):
        one(index)
        return carry

    lax.fori_loop(0, count, step, 0)


def remote(source, target, send_sem, recv_sem, device):
    return pltpu.make_async_remote_copy(
        src_ref=source,
        dst_ref=target,
        send_sem=send_sem,
        recv_sem=recv_sem,
        device_id=device,
        device_id_type=MESH,
    )


def to_column(row):
    count = row.shape[1]
    eye = iota((count, count), 0) == iota((count, count), 1)
    whole = jnp.broadcast_to(row, (count, count))
    return jnp.sum(jnp.where(eye, whole, jnp.zeros_like(whole)), axis=1, keepdims=True)


def to_row(column):
    count = column.shape[0]
    eye = iota((count, count), 0) == iota((count, count), 1)
    whole = jnp.broadcast_to(column, (count, count))
    return jnp.sum(jnp.where(eye, whole, jnp.zeros_like(whole)), axis=0, keepdims=True)


def total(values):
    return jnp.sum(values, axis=1, keepdims=True)


def step_kernel(
    sections,
    replicas,
    parts,
    per_pair,
    token_ids_ref,
    next_ids_ref,
    main_cot_ref,
    mtp_cot_ref,
    gain_ref,
    mtp_gain_ref,
    table_hbm,
    gate_hbm,
    up_hbm,
    down_hbm,
    sums_ref,
    lid_ref,
    over_ref,
    table,
    ids_ref,
    first,
    rank,
    lid,
    onehot,
    send,
    recv,
    rows_ref,
    grad_ref,
    gu,
    down,
    relay_gu,
    relay_down,
    part_out,
    part_in,
    early_out,
    early_in,
    narrow_in,
    wide_in,
    stat_in,
    mixed_all,
    cot_all,
    back_out,
    back_in,
    back_relay,
    cross,
    hold,
    table_sem,
    local_sem,
    row_send,
    row_recv,
    sum_send,
    sum_recv,
    weight_local,
    local_weight,
    weight_send,
    weight_recv,
    relay_send,
    relay_recv,
    part_send,
    part_recv,
    early_send,
    early_recv,
    wide_send,
    wide_recv,
    narrow_send,
    narrow_recv,
    stat_send,
    stat_recv,
    cross_send,
    cross_recv,
    mixed_send,
    mixed_recv,
    cot_send,
    cot_recv,
    back_send,
    back_recv,
    back_relay_send,
    back_relay_recv,
):
    section = lax.axis_index("section")
    replica = lax.axis_index("dp")
    part = lax.axis_index("mp")
    count = sections * replicas
    me = section * replicas + replica
    vocab_rows, width = table_hbm.shape
    hidden = gate_hbm.shape[1]
    batches = token_ids_ref.shape[0]
    tokens = ids_ref.shape[1]
    run = tokens // batches
    model_width = parts * width
    slots = count * per_pair
    ring = parts // 2
    load = pltpu.make_async_copy(table_hbm, table, table_sem)
    load.start()

    def column_peer(step):
        there = step // replicas
        other = lax.rem(replica + 1 + step, replicas)
        return there * replicas + other, (there, other, part)

    def away(ahead, across):
        return lax.rem(part // 2 + ahead, ring) * 2 + lax.rem(part + across, 2)

    def row_peer(step):
        ahead = jnp.where(
            step < 2,
            1 + step * (ring - 2),
            jnp.where(step == 2, 0, jnp.where(step < 5, 1 + (step - 3) * (ring - 2), 2)),
        )
        across = jnp.where(step < 2, 0, jnp.where(step < 5, 1, step - 5))
        other = away(ahead, across)
        return other, (section, replica, other)

    barrier = pltpu.get_barrier_semaphore()

    def greet_column(step):
        other, device = column_peer(step)

        @pl.when(other != me)
        def _():
            pl.semaphore_signal(barrier, inc=1, device_id=device, device_id_type=MESH)

    def greet_row(step):
        other = lax.rem(part + 1 + lax.rem(step, parts - 1), parts)
        there = jnp.where(step < parts - 1, section, 1 - section)
        pl.semaphore_signal(
            barrier, inc=1, device_id=(there, replica, other), device_id_type=MESH
        )

    loop(count, greet_column)
    loop(2 * (parts - 1), greet_row)

    rows_of = 2 * batches
    row_index = lax.rem(iota((rows_of, tokens), 0), batches)
    own_run = iota((rows_of, tokens), 1) // run == row_index
    for group in range(replicas // batches):
        columns = pl.ds(group * tokens, tokens)
        both = jnp.concatenate(
            [token_ids_ref[:, columns], next_ids_ref[:, columns]], axis=0
        ).astype(F32)
        turned = [both] + [pltpu.roll(both, shift * run, 1) for shift in range(1, batches)]
        for inner in range(batches):
            value = jnp.zeros_like(both)
            for shift in range(batches):
                wanted = own_run & (lax.rem(row_index - inner + batches, batches) == shift)
                value = jnp.where(wanted, turned[shift], value)
            index = group * batches + inner
            ids_ref[index : index + 1, :] = jnp.sum(value[:batches], axis=0, keepdims=True)
            ids_ref[replicas + index : replicas + index + 1, :] = jnp.sum(
                value[batches:], axis=0, keepdims=True
            )

    earlier = iota((tokens, tokens), 0) < iota((tokens, tokens), 1)

    def find_first(step):
        for inner in range(4):
            index = pl.ds(step * 4 + inner, 1)
            row = ids_ref[index, :]
            same = (to_column(row) == row) & earlier
            seen = jnp.max(jnp.where(same, 1.0, 0.0), axis=0, keepdims=True)
            first[index, :] = 1.0 - seen

    loop(replicas // 4, find_first)
    pl.semaphore_wait(barrier, count - 1 + 2 * (parts - 1))

    def weight_source(target):
        features = pl.ds(pl.multiple_of(target * width, width), width)
        return gate_hbm.at[features, :], up_hbm.at[features, :], down_hbm.at[:, features]

    def weight_slot(origin):
        return (
            gu.at[origin, :, pl.ds(0, hidden)],
            gu.at[origin, :, pl.ds(hidden, hidden)],
            down.at[origin],
        )

    def relay_slot(way):
        return (
            relay_gu.at[way, :, pl.ds(0, hidden)],
            relay_gu.at[way, :, pl.ds(hidden, hidden)],
            relay_down.at[way],
        )

    def direct_copy(kind, step):
        other, device = row_peer(step)
        return remote(
            weight_source(other)[kind],
            weight_slot(part)[kind],
            weight_send.at[kind, step],
            weight_recv.at[kind, part],
            device,
        )

    def relay_copy(kind, way):
        final = away(2, way)
        return remote(
            weight_source(final)[kind],
            relay_slot(way)[kind],
            weight_send.at[kind, parts - 3 + way],
            relay_recv.at[kind, way],
            (section, replica, away(1 + way * (ring - 2), 0)),
        )

    def forward_copy(kind, way):
        origin = away(ring - 1 - way * (ring - 2), 0)
        final = away(1 + way * (ring - 2), way)
        return remote(
            relay_slot(way)[kind],
            weight_slot(origin)[kind],
            relay_send.at[kind, way],
            weight_recv.at[kind, origin],
            (section, replica, final),
        )

    def own_weight(kind):
        return pltpu.make_async_copy(
            weight_source(part)[kind], weight_slot(part)[kind], weight_local.at[kind]
        )

    def local_weights(then):
        def one(target):
            for kind, source in enumerate(weight_source(target)):
                then(
                    pltpu.make_async_copy(
                        source, weight_slot(target)[kind], local_weight.at[kind, target]
                    )
                )

        loop(parts, one)

    def weights_start():
        for kind in range(3):
            for way in range(2):
                relay_copy(kind, way).start()
            loop(parts - 3, lambda step: direct_copy(kind, step).start())
        for kind in range(3):
            own_weight(kind).start()

    def relay_on(kinds):
        for kind in kinds:
            for way in range(2):
                relay_copy(kind, way).wait_recv()
                forward_copy(kind, way).start()

    def weight_wait(kind, step):
        other, device = row_peer(step)
        remote(
            weight_slot(other)[kind],
            weight_slot(other)[kind],
            weight_send.at[kind, step],
            weight_recv.at[kind, other],
            device,
        ).wait_recv()

    @pl.when(section == 0)
    def _():
        weights_start()

    @pl.when(section == 1)
    def _():
        local_weights(lambda copy: copy.start())

    def shard_of(rows):
        return jnp.floor(rows * (1.0 / vocab_rows))

    triangle = jnp.where(earlier, 1.0, 0.0).astype(BF)
    me_f = me.astype(F32)
    group = min(replicas, max(1, 2 * tokens // per_pair))

    def row_copy(step):
        other, device = column_peer(step)
        return remote(send.at[other], recv.at[me], row_send.at[step], row_recv.at[me], device)

    def send_rows(half):
        half_rows = pl.ds(half * replicas, replicas)
        mine = jnp.where(shard_of(ids_ref[half_rows, :]) == me_f, first[half_rows, :], 0.0)
        rank[...] = jnp.where(mine > 0.0, dot(mine.astype(BF), triangle), -1.0)

        def find_lid(step):
            for inner in range(4):
                index = step * 4 + inner
                there = half * replicas + index
                row = ids_ref[pl.ds(there, 1), :] - (me_f * vocab_rows - 1.0)
                picks = rank[pl.ds(index, 1), :].astype(jnp.int32) == iota(
                    (per_pair, tokens), 0
                )
                found = total(jnp.where(picks, jnp.broadcast_to(row, picks.shape), 0.0))
                lid[pl.ds(pl.multiple_of(there * per_pair, per_pair), per_pair), :] = (
                    jnp.broadcast_to(found - 1.0, (per_pair, tokens)).astype(jnp.int32)
                )

        loop(replicas // 4, find_lid)

        def chunk(block):
            base = half * replicas + block * group

            def mark(step):
                other = column_peer(base + step)[0]
                wanted = lid[
                    pl.ds(pl.multiple_of(other * per_pair, per_pair), per_pair), :
                ]
                there = pl.ds(pl.multiple_of(step * per_pair, per_pair), per_pair)
                for lane in range(vocab_rows // tokens):
                    hit = wanted == iota(wanted.shape, 1) + lane * tokens
                    onehot[there, pl.ds(lane * tokens, tokens)] = jnp.where(
                        hit, 1.0, 0.0
                    ).astype(BF)

            loop(group, mark)
            found = dot(onehot[...], table[...]).astype(BF)
            for step in range(group):
                other = column_peer(base + step)[0]
                send[other] = found[step * per_pair : (step + 1) * per_pair]

            def go(step):
                @pl.when(column_peer(base + step)[0] != me)
                def _():
                    row_copy(base + step).start()

            loop(group, go)

        if group == replicas:
            chunk(0)
        else:
            loop(replicas // group, chunk)

    load.wait()
    send_rows(0)
    loop(replicas // 4, lambda step: find_first(step + replicas // 4))
    send_rows(1)
    recv[me] = send[me]

    @pl.when(section == 0)
    def _():
        relay_on((0, 1))

    shard = shard_of(ids_ref[...])

    def fill(step, most):
        for inner in range(4):
            held = jnp.where(shard == (step * 4 + inner).astype(F32), first[...], 0.0)
            most = jnp.maximum(most, total(held))
        return most

    most = lax.fori_loop(0, count // 4, fill, jnp.zeros((count, 1), F32))
    over_ref[...] = jnp.broadcast_to(jnp.max(most, axis=0, keepdims=True), over_ref.shape)
    eye = iota((tokens, tokens), 0) == iota((tokens, tokens), 1)

    def turn(block):
        rows = pl.ds(pl.multiple_of(block * tokens, tokens), tokens)
        row = jnp.sum(jnp.where(eye, lid[rows, :], 0), axis=0, keepdims=True)
        lid_ref[:, rows] = jnp.broadcast_to(row, (8, tokens))

    loop(slots // tokens, turn)
    own_row = ids_ref[pl.ds(me, 1), :]
    own_first = first[pl.ds(me, 1), :]
    own_column = to_column(own_row)
    shard_row = shard_of(own_row)
    counted = (shard_of(own_column) == shard_row) & earlier & (to_column(own_first) > 0.0)
    slot_row = shard_row * per_pair + jnp.sum(
        jnp.where(counted, 1.0, 0.0), axis=0, keepdims=True
    )
    leads = (own_column == own_row) & (own_first > 0.0)
    slot_column = total(jnp.where(leads, jnp.broadcast_to(slot_row, leads.shape), 0.0))

    def row_wait(step):
        other, device = column_peer(step)

        @pl.when(other != me)
        def _():
            remote(
                send.at[me], recv.at[other], row_send.at[step], row_recv.at[other], device
            ).wait_recv()

    loop(count, row_wait)
    slot_of = slot_column.astype(jnp.int32)
    spread = jnp.where(slot_of == iota((tokens, slots), 1), 1.0, 0.0).astype(BF)
    rows_ref[...] = dot(spread, recv[...].reshape(slots, width)).astype(BF)

    features = pl.ds(pl.multiple_of(part * width, width), width)
    gain = gain_ref[0:1, features]
    gain_main = mtp_gain_ref[0:1, features]
    gain_next = mtp_gain_ref[1:2, features]

    def inverse(sum_of_squares):
        return lax.rsqrt(sum_of_squares / model_width + EPS)

    def lanes(index, size):
        return pl.ds(pl.multiple_of(index * size, size), size)

    def put_stats(slot, columns):
        rows = [to_row(column) for column in columns]
        rows = rows + [jnp.zeros_like(rows[0])] * (8 - len(rows))
        stat_in[slot, part] = jnp.concatenate(rows, axis=0)

    def get_stats(slot, number):
        value = stat_in[slot, 0]
        for index in range(1, parts):
            value = value + stat_in[slot, index]
        return [to_column(value[index : index + 1, :]) for index in range(number)]

    def stat_copy(slot, step):
        return remote(
            stat_in.at[slot, part],
            stat_in.at[slot, part],
            stat_send.at[slot, step],
            stat_recv.at[slot, part],
            row_peer(step)[1],
        )

    def share_stats(slot):
        loop(parts - 1, lambda step: stat_copy(slot, step).start())

    def wait_stats(slot):
        def one(step):
            other, device = row_peer(step)
            remote(
                stat_in.at[slot, other],
                stat_in.at[slot, other],
                stat_send.at[slot, step],
                stat_recv.at[slot, other],
                device,
            ).wait()

        loop(parts - 1, one)

    def tell_copy(step):
        other = lax.rem(part + step, parts)
        return remote(
            stat_in.at[1, part],
            stat_in.at[1, part],
            stat_send.at[1, step],
            stat_recv.at[1, part],
            (1 - section, replica, other),
        )

    def gate_up_start(normed):
        def partial(other):
            part_out[other] = dot(normed, gu[other]).astype(BF)

        def one(step):
            other, device = row_peer(step)
            weight_wait(0, step)
            weight_wait(1, step)
            partial(other)
            remote(
                part_out.at[other],
                part_in.at[part],
                part_send.at[step],
                part_recv.at[part],
                device,
            ).start()

        loop(parts - 1, one)
        own_weight(0).wait()
        own_weight(1).wait()
        partial(part)

    def gate_up_wait():
        def one(step, value):
            other, device = row_peer(step)
            remote(
                part_in.at[other],
                part_in.at[other],
                part_send.at[step],
                part_recv.at[other],
                device,
            ).wait()
            return value + part_in[other].astype(F32)

        return lax.fori_loop(0, parts - 1, one, part_out[part].astype(F32))

    def down_wait():
        loop(parts - 1, lambda step: weight_wait(2, step))
        own_weight(2).wait()

    def grad_hidden_start(grad):
        early_out[...] = dot_t(grad, down[...].reshape(parts * hidden, width)).astype(BF)

        def one(step):
            other, device = row_peer(step)
            remote(
                early_out.at[:, lanes(other, hidden)],
                early_in.at[part],
                early_send.at[step],
                early_recv.at[part],
                device,
            ).start()

        loop(parts - 1, one)

    def grad_hidden_wait():
        def one(step, value):
            other, device = row_peer(step)
            remote(
                early_in.at[other],
                early_in.at[other],
                early_send.at[step],
                early_recv.at[other],
                device,
            ).wait()
            return value + early_in[other].astype(F32)

        return lax.fori_loop(
            0, parts - 1, one, early_out[:, lanes(part, hidden)].astype(F32)
        )

    def share_columns(whole, size, send_sem, recv_sem):
        def start(step):
            device = row_peer(step)[1]
            own = whole.at[:, lanes(part, size)]
            remote(own, own, send_sem.at[step], recv_sem.at[part], device).start()

        def wait(step):
            other, device = row_peer(step)
            theirs = whole.at[:, lanes(other, size)]
            remote(theirs, theirs, send_sem.at[step], recv_sem.at[other], device).wait()

        loop(parts - 1, start)
        loop(parts - 1, wait)

    def slopes(gate, up, grad_hidden):
        sigmoid = jax.nn.sigmoid(gate)
        grad_gate = grad_hidden * up * sigmoid * (1.0 + gate * (1.0 - sigmoid))
        grad_up = grad_hidden * gate * sigmoid
        return jnp.concatenate([grad_gate, grad_up], axis=1).astype(BF)

    def block_copy(whole, send_sem, recv_sem, block, step, device):
        return remote(
            whole.at[block], whole.at[block], send_sem.at[step], recv_sem.at[block], device
        )

    def gather_blocks(whole, send_sem, recv_sem, use):
        up_one = (section, replica, away(1, 0))
        down_one = (section, replica, away(ring - 1, 0))
        beside = (section, replica, away(0, 1))
        plan = [
            (away(0, 0), (up_one, down_one, beside)),
            (away(0, 1), (up_one, down_one)),
            (away(ring - 1, 0), (up_one,)),
            (away(1, 0), ()),
            (away(1, 1), (down_one,)),
            (away(ring - 1, 1), ()),
            (away(2, 0), ()),
            (away(2, 1), ()),
        ]
        step = 0
        sent = []
        for position, (block, devices) in enumerate(plan):
            if position > 0:
                block_copy(whole, send_sem, recv_sem, block, 0, beside).wait_recv()
            for device in devices:
                copy = block_copy(whole, send_sem, recv_sem, block, step, device)
                copy.start()
                sent.append(copy)
                step += 1
            use(block)
        for copy in sent:
            copy.wait_send()

    def gather_dot(whole, send_sem, recv_sem, product):
        held = []

        def use(block):
            held.append(product(whole[block], block))

        gather_blocks(whole, send_sem, recv_sem, use)
        value = held[0]
        for other in held[1:]:
            value = value + other
        return value

    def return_blocks(terms):
        up_one = (section, replica, away(1, 0))
        down_one = (section, replica, away(ring - 1, 0))
        plan = [
            (away(2, 0), up_one, 0),
            (away(2, 1), down_one, 1),
            (away(1, 1), None, None),
            (away(ring - 1, 1), None, None),
            (away(1, 0), None, None),
            (away(ring - 1, 0), None, None),
            (away(0, 1), None, None),
        ]
        sent = []
        for step, (block, device, way) in enumerate(plan):
            back_out[block] = dot_t(terms, gu[block]).astype(BF)
            target = back_in.at[part] if way is None else back_relay.at[way]
            arrived = back_recv.at[part] if way is None else back_relay_recv.at[way]
            copy = remote(
                back_out.at[block],
                target,
                back_send.at[step],
                arrived,
                (section, replica, block) if device is None else device,
            )
            copy.start()
            sent.append(copy)
        own = dot_t(terms, gu[part])
        for way in range(2):
            origin = away(ring - 1 - way * (ring - 2), 0)
            final = away(1 + way * (ring - 2), way)
            sent[way].wait_recv()
            copy = remote(
                back_relay.at[way],
                back_in.at[origin],
                back_relay_send.at[way],
                back_recv.at[origin],
                (section, replica, final),
            )
            copy.start()
            sent.append(copy)
        for block in (
            away(0, 1),
            away(1, 0),
            away(ring - 1, 0),
            away(1, 1),
            away(ring - 1, 1),
            away(2, 0),
            away(2, 1),
        ):
            remote(
                back_in.at[block],
                back_in.at[block],
                back_send.at[0],
                back_recv.at[block],
                (section, replica, block),
            ).wait_recv()
            own = own + back_in[block].astype(F32)
        for copy in sent:
            copy.wait_send()
        return own * gain

    over = remote(
        cross.at[0], cross.at[1], cross_send, cross_recv, (1 - section, replica, part)
    )

    @pl.when(section == 0)
    def _():
        rows = rows_ref[...].astype(F32)
        put_stats(0, [total(rows * rows)])
        share_stats(0)
        gate_up_start((rows * gain).astype(BF))
        relay_on((2,))
        wait_stats(0)
        scale = inverse(get_stats(0, 1)[0])
        whole = gate_up_wait() * scale
        hold[...] = whole
        gate = whole[:, :hidden]
        up = whole[:, hidden:]
        narrow_in[:, lanes(part, hidden)] = (gate * jax.nn.sigmoid(gate) * up).astype(BF)
        share_columns(narrow_in, hidden, narrow_send, narrow_recv)
        down_wait()
        out = rows_ref[...].astype(F32) + dot(narrow_in[...], down[...].reshape(parts * hidden, width))
        cross[0] = out.astype(BF)
        over.start()
        main = cross[0].astype(F32)
        put_stats(1, [total(main * main)])
        loop(parts, lambda step: tell_copy(step).start())
        loop(parts, lambda step: tell_copy(step).wait_send())
        over.wait()
        grad = cross[1]
        grad_hidden_start(grad)
        grad_hidden = grad_hidden_wait()
        whole = hold[...]
        wide_in[:, lanes(part, 2 * hidden)] = slopes(
            whole[:, :hidden], whole[:, hidden:], grad_hidden
        )
        share_columns(wide_in, 2 * hidden, wide_send, wide_recv)
        scaled = dot_t(wide_in[:, pl.ds(0, 2 * hidden)], gu[0])
        for index in range(1, parts):
            scaled = scaled + dot_t(
                wide_in[:, pl.ds(index * 2 * hidden, 2 * hidden)], gu[index]
            )
        scaled = scaled * gain
        rows = rows_ref[...].astype(F32)
        put_stats(2, [total(rows * scaled)])
        share_stats(2)
        wait_stats(2)
        mean = get_stats(2, 1)[0] / model_width
        scale = inverse(get_stats(0, 1)[0])
        result = grad.astype(F32) + scale * scaled - rows * (scale * scale * scale * mean)
        grad_ref[...] = result.astype(BF)

    @pl.when(section == 1)
    def _():
        rows = rows_ref[...].astype(F32)
        put_stats(0, [total(rows * rows)])
        share_stats(0)
        local_weights(lambda copy: copy.wait())
        cot_all[part] = mtp_cot_ref[...]
        grad_hidden = gather_dot(
            cot_all, cot_send, cot_recv, lambda block, index: dot_t(block, down[index])
        )
        wait_stats(0)
        scale_next = inverse(get_stats(0, 1)[0])

        def heard(index):
            remote(
                stat_in.at[1, index],
                stat_in.at[1, index],
                stat_send.at[1, 0],
                stat_recv.at[1, index],
                (1 - section, replica, part),
            ).wait_recv()

        loop(parts, heard)
        over.wait_recv()
        scale_main = inverse(get_stats(1, 1)[0])
        main = cross[1].astype(F32)
        mixed = (main * scale_main * gain_main + rows * scale_next * gain_next).astype(BF)
        mixed = mixed.astype(F32)
        put_stats(2, [total(mixed * mixed)])
        share_stats(2)
        mixed_all[part] = (mixed * gain).astype(BF)
        whole = gather_dot(
            mixed_all, mixed_send, mixed_recv, lambda block, index: dot(block, gu[index])
        )
        wait_stats(2)
        scale = inverse(get_stats(2, 1)[0])
        whole = whole * scale
        scaled = return_blocks(slopes(whole[:, :hidden], whole[:, hidden:], grad_hidden))
        cot = mtp_cot_ref[...].astype(F32)
        next_weighted = rows * gain_next
        main_weighted = main * gain_main
        put_stats(
            3,
            [
                total(mixed * scaled),
                total(next_weighted * scaled),
                total(next_weighted * mixed),
                total(next_weighted * cot),
                total(main_weighted * scaled),
                total(main_weighted * mixed),
                total(main_weighted * cot),
            ],
        )
        share_stats(3)
        wait_stats(3)
        s1, s2, s3, s4, s5, s6, s7 = get_stats(3, 7)
        slope = scale * scale * scale * (s1 / model_width)
        grad_mixed = cot + scale * scaled - mixed * slope
        mean_next = (s4 + scale * s2 - slope * s3) / model_width
        mean_main = (s7 + scale * s5 - slope * s6) / model_width
        grad_main = (
            main_cot_ref[...].astype(F32)
            + scale_main * (gain_main * grad_mixed)
            - main * (scale_main * scale_main * scale_main * mean_main)
        )
        cross[0] = grad_main.astype(BF)
        over.start()
        grad_next = scale_next * (gain_next * grad_mixed) - rows * (
            scale_next * scale_next * scale_next * mean_next
        )
        grad_ref[...] = grad_next.astype(BF)
        over.wait_send()

    def row_done(step):
        @pl.when(column_peer(step)[0] != me)
        def _():
            row_copy(step).wait_send()

    loop(count, row_done)
    slot_back = to_row(slot_column).astype(jnp.int32)
    group_rows = group * per_pair

    def pack(block):
        hit = slot_back == iota((group_rows, tokens), 0) + block * group_rows
        found = dot(jnp.where(hit, 1.0, 0.0).astype(BF), grad_ref[...]).astype(BF)
        send[pl.ds(block * group, group)] = found.reshape(group, per_pair, width)

    loop(count // group, pack)

    def sum_copy(step):
        other, device = column_peer(step)
        return remote(
            send.at[other], sums_ref.at[me], sum_send.at[step], sum_recv.at[me], device
        )

    def sum_start(step):
        @pl.when(column_peer(step)[0] != me)
        def _():
            sum_copy(step).start()

    loop(count, sum_start)
    sums_ref[me] = send[me]

    @pl.when(section == 0)
    def _():
        for kind in range(3):
            for way in range(2):
                relay_copy(kind, way).wait_send()
                forward_copy(kind, way).wait_send()
            loop(parts - 3, lambda step: direct_copy(kind, step).wait_send())

    def sum_wait(step):
        other, device = column_peer(step)

        @pl.when(other != me)
        def _():
            remote(
                send.at[other],
                sums_ref.at[other],
                sum_send.at[step],
                sum_recv.at[other],
                device,
            ).wait()

    loop(count, sum_wait)


def place_kernel(lid_ref, sums_ref, out_ref):
    rows = out_ref.shape[0]
    slots = sums_ref.shape[0]
    base = pl.program_id(0) * rows
    hit = lid_ref[0:1, :] == iota((rows, slots), 0) + base
    out_ref[...] = dot(jnp.where(hit, 1.0, 0.0).astype(BF), sums_ref[...]).astype(BF)


def vmem():
    return pl.BlockSpec(memory_space=pltpu.VMEM)


def anywhere():
    return pl.BlockSpec(memory_space=pl.ANY)


def dma(*shape):
    return pltpu.SemaphoreType.DMA(shape)


def train_step(
    per_pair,
    token_ids,
    next_ids,
    embed_table,
    norm_gain,
    w_gate,
    w_up,
    w_down,
    mtp_gain,
    main_cot,
    mtp_cot,
):
    sections = lax.axis_size("section")
    replicas = lax.axis_size("dp")
    parts = lax.axis_size("mp")
    count = sections * replicas
    batches = token_ids.shape[0]
    tokens = batches * (token_ids.shape[1] // replicas)
    vocab_rows, width = embed_table.shape
    hidden = w_gate.shape[2]
    slots = count * per_pair
    picked = min(replicas * per_pair, max(2 * tokens, per_pair))
    block = pltpu.VMEM((parts, tokens, width), BF)
    one = pltpu.SemaphoreType.DMA
    return pl.pallas_call(
        functools.partial(step_kernel, sections, replicas, parts, per_pair),
        out_shape=(
            jax.ShapeDtypeStruct((count, per_pair, width), BF),
            jax.ShapeDtypeStruct((8, slots), jnp.int32),
            jax.ShapeDtypeStruct((8, 128), F32),
        ),
        in_specs=[vmem()] * 6 + [anywhere()] * 4,
        out_specs=(vmem(), vmem(), vmem()),
        scratch_shapes=[
            pltpu.VMEM((vocab_rows, width), BF),
            pltpu.VMEM((count, tokens), F32),
            pltpu.VMEM((count, tokens), F32),
            pltpu.VMEM((replicas, tokens), F32),
            pltpu.VMEM((slots, tokens), jnp.int32),
            pltpu.VMEM((picked, vocab_rows), BF),
            pltpu.VMEM((count, per_pair, width), BF),
            pltpu.VMEM((count, per_pair, width), BF),
            pltpu.VMEM((tokens, width), BF),
            pltpu.VMEM((tokens, width), BF),
            pltpu.VMEM((parts, width, 2 * hidden), BF),
            pltpu.VMEM((parts, hidden, width), BF),
            pltpu.VMEM((2, width, 2 * hidden), BF),
            pltpu.VMEM((2, hidden, width), BF),
            pltpu.VMEM((parts, tokens, 2 * hidden), BF),
            pltpu.VMEM((parts, tokens, 2 * hidden), BF),
            pltpu.VMEM((tokens, parts * hidden), BF),
            pltpu.VMEM((parts, tokens, hidden), BF),
            pltpu.VMEM((tokens, parts * hidden), BF),
            pltpu.VMEM((tokens, parts * 2 * hidden), BF),
            pltpu.VMEM((4, parts, 8, tokens), F32),
            block,
            block,
            block,
            block,
            pltpu.VMEM((2, tokens, width), BF),
            pltpu.VMEM((2, tokens, width), BF),
            pltpu.VMEM((tokens, 2 * hidden), F32),
            one,
            one,
            dma(count),
            dma(count),
            dma(count),
            dma(count),
            dma(3),
            dma(3, parts),
            dma(3, parts),
            dma(3, parts),
            dma(3, 2),
            dma(3, 2),
        ]
        + [dma(parts)] * 8
        + [dma(4, parts)] * 2
        + [one] * 2
        + [dma(parts)] * 6
        + [dma(2)] * 2,
        compiler_params=pltpu.CompilerParams(
            collective_id=0 if per_pair == FEW_SLOTS else 1,
            has_side_effects=True,
            vmem_limit_bytes=60 << 20,
        ),
        name=f"train_step_{per_pair}",
    )(
        token_ids,
        next_ids,
        main_cot.reshape(tokens, width),
        mtp_cot.reshape(tokens, width),
        norm_gain,
        mtp_gain,
        embed_table,
        w_gate[0],
        w_up[0],
        w_down[0],
    )


def place(lid_row, sums, vocab_rows):
    width = sums.shape[-1]
    slots = lid_row.shape[1]
    block = vocab_rows // 8
    return pl.pallas_call(
        place_kernel,
        grid=(vocab_rows // block,),
        out_shape=jax.ShapeDtypeStruct((vocab_rows, width), BF),
        in_specs=[
            pl.BlockSpec((8, slots), lambda i: (0, 0)),
            pl.BlockSpec((slots, width), lambda i: (0, 0)),
        ],
        out_specs=pl.BlockSpec((block, width), lambda i: (i, 0)),
        compiler_params=pltpu.CompilerParams(vmem_limit_bytes=56 << 20),
        name="place_rows",
    )(lid_row, sums.reshape(slots, width))


def body(*arguments):
    vocab_rows = arguments[2].shape[0]
    positions = arguments[0].shape[0] * (arguments[0].shape[1] // lax.axis_size("dp"))
    sums, lid_row, most = train_step(FEW_SLOTS, *arguments)

    def few(sums, lid_row, *given):
        return place(lid_row, sums, vocab_rows)

    def many(sums, lid_row, *given):
        sums, lid_row, most = train_step(positions, *given)
        return place(lid_row, sums, vocab_rows)

    return lax.cond(most[0, 0] <= FEW_SLOTS, few, many, sums, lid_row, *arguments)


def solution(mesh):
    return jax.shard_map(
        body,
        mesh=mesh,
        in_specs=(
            P(),
            P(),
            P(("section", "dp"), "mp"),
            P("section", None),
            P("section", None, "mp"),
            P("section", None, "mp"),
            P("section", "mp", None),
            P(),
            P(None, "dp", "mp"),
            P(None, "dp", "mp"),
        ),
        out_specs=P(("section", "dp"), "mp"),
        check_vma=False,
    )
```

time: 178 us -> 153 us (0.86)
  between operations: 14.1 us -> 0.71 us
  Pallas kernels: 160 us -> 149 us
    pallas_call x1, Pallas kernels: 154 us -> 144 us  [train_step(): pl.pallas_call(functools.partial(step_kernel, sections, replicas, parts,...]
    unnamed x10 -> x8, local copies, waits for them, and re-layouts: 0.02 us -> 1.84 us
where the time goes in v3:
time: 153 us
  Pallas kernels  149 us (97%)
  local copies, waits for them, and re-layouts  3.04 us (2%)
    pallas_call x1, Pallas kernels, train_step(): pl.pallas_call(functools.partial(step_kernel, sections, replicas, parts,...  144 us
    pallas_call x1, Pallas kernels, place(): pl.pallas_call(place_kernel, grid=(vocab_rows // block,), out_shape=jax.S...  4.79 us

profile of v3, /device:TPU:1, one launch (start us, length us, event | category | flops | bytes accessed | tf_op | source)
XLA Modules:
  0.0 153.2 jit_solution(8796077925289187583)
XLA Ops:
  0.0 0.0 copy-start
  0.0 0.0 copy-start.2
  0.0 0.0 copy-start.3
  0.0 144.4 %train_step_16.1 = (bf16[32,16,896]{2,1,0:T(8,128)(2,1)}, s32[8,512]{1,0:T(8,128)}, f32[8,128]{1,0:T(8,128)}) custom-call(s32[4,512]{1,0:T(4,128)} %token_ids_ref.1, s32[4,512]{1,0:T(4,128)} %next_ids_ref.1, bf16[128,896]{1,0:T(8,128)(2,1)} %bitcast.21, bf16[128,896]{1,0:T(8,128)(2,1)} %bitcast.23, f32[1,7168]{1,0:T(1,128)} %gain_ref.1, ...), custom_call_target="tpu_custom_call" | custom-call | tf_op jit(solution)/shard_map/train_step_16/pallas_call | solution.py:923
  144.4 1.2 slice.3
  146.3 0.0 copy-done
  146.3 0.0 copy-done.2
  146.3 0.0 copy-done.3
  146.3 5.0 %conditional.1 = (bf16[2048,896]{1,0:T(8,128)(2,1)S(1)}) conditional(s32[]{:T(128)} %bitcast.12, (bf16[4,32,896]{2,1,0:T(8,128)(2,1)S(1)}, bf16[4,32,896]{2,1,0:T(8,128)(2,1)S(1)}, bf16[1,7168,128]{2,1,0:T(8,128)(2,1)}, bf16[1,7168,128]{2,1,0:T(8,128)(2,1)}, bf16[1,128,7168]{2,1,0:T(8,128)(2,1)}, /*index=5*/s32[4,512]{1,0:T(4,128)}, ...), branch_computations={%region_0.0_spmd, %region_1.0_spmd} | conditional | bytes 8 | solution.py:1029
  146.6 4.8 %place_rows.3 = bf16[2048,896]{1,0:T(8,128)(2,1)S(1)} custom-call(s32[8,512]{1,0:T(8,128)} %get-tuple-element.44.lid_ref, bf16[512,896]{1,0:T(8,128)(2,1)} %bitcast.20), custom_call_target="tpu_custom_call" | custom-call | tf_op jit(solution)/shard_map/cond/branch_1_fun/place_rows/pallas_call | solution.py:1003
  151.3 0.0 copy-start.1
  151.4 1.8 %copy-done.1 = bf16[2048,896]{1,0:T(8,128)(2,1)} copy-done((bf16[2048,896]{1,0:T(8,128)(2,1)}, bf16[2048,896]{1,0:T(8,128)(2,1)S(1)}, u32[]{:S(2)}) %copy-start.1) | copy-done | bytes 3670040
Async XLA Ops:
  0.0 146.3 %copy-start = (bf16[2048,896]{1,0:T(8,128)(2,1)S(1)}, bf16[2048,896]{1,0:T(8,128)(2,1)}, u32[]{:S(2)}) copy-start(bf16[2048,896]{1,0:T(8,128)(2,1)} %table_hbm.1) | copy-start | bytes 11010052
  0.0 146.3 %copy-start.2 = (bf16[4,32,896]{2,1,0:T(8,128)(2,1)S(1)}, bf16[4,32,896]{2,1,0:T(8,128)(2,1)}, u32[]{:S(2)}) copy-start(bf16[4,32,896]{2,1,0:T(8,128)(2,1)} %param.20) | copy-start | bytes 688132
  0.0 146.3 %copy-start.3 = (bf16[4,32,896]{2,1,0:T(8,128)(2,1)S(1)}, bf16[4,32,896]{2,1,0:T(8,128)(2,1)}, u32[]{:S(2)}) copy-start(bf16[4,32,896]{2,1,0:T(8,128)(2,1)} %param.21) | copy-start | bytes 688132
  151.3 1.8 %copy-start.1 = (bf16[2048,896]{1,0:T(8,128)(2,1)}, bf16[2048,896]{1,0:T(8,128)(2,1)S(1)}, u32[]{:S(2)}) copy-start(bf16[2048,896]{1,0:T(8,128)(2,1)S(1)} %get-tuple-element.55) | copy-start | bytes 11010052

commit v4 on v3

--- a/solution.py
+++ b/solution.py
@@ -9,7 +9,7 @@
 
 EPS = 1e-06
 MESH = pl.DeviceIdType.MESH
-FEW_SLOTS = 16
+FEW_SLOTS = 32
 BF = jnp.bfloat16
 F32 = jnp.float32
 COLS = (((1,), (1,)), ((), ()))
@@ -89,6 +89,8 @@
     lid,
     onehot,
     send,
+    swap_out,
+    swap_in,
     recv,
     rows_ref,
     grad_ref,
@@ -112,10 +114,14 @@
     hold,
     table_sem,
     local_sem,
+    swap_send,
+    swap_recv,
     row_send,
     row_recv,
     sum_send,
     sum_recv,
+    pass_send,
+    pass_recv,
     weight_local,
     local_weight,
     weight_send,
@@ -154,15 +160,17 @@
     tokens = ids_ref.shape[1]
     run = tokens // batches
     model_width = parts * width
-    slots = count * per_pair
+    half = per_pair // 2
+    slots = replicas * per_pair
     ring = parts // 2
     load = pltpu.make_async_copy(table_hbm, table, table_sem)
     load.start()
 
     def column_peer(step):
-        there = step // replicas
         other = lax.rem(replica + 1 + step, replicas)
-        return there * replicas + other, (there, other, part)
+        return other, (section, other, part)
+
+    partner = (1 - section, replica, part)
 
     def away(ahead, across):
         return lax.rem(part // 2 + ahead, ring) * 2 + lax.rem(part + across, 2)
@@ -180,21 +188,19 @@
     barrier = pltpu.get_barrier_semaphore()
 
     def greet_column(step):
-        other, device = column_peer(step)
-
-        @pl.when(other != me)
-        def _():
-            pl.semaphore_signal(barrier, inc=1, device_id=device, device_id_type=MESH)
+        device = column_peer(step)[1]
+        pl.semaphore_signal(barrier, inc=1, device_id=device, device_id_type=MESH)
 
     def greet_row(step):
-        other = lax.rem(part + 1 + lax.rem(step, parts - 1), parts)
+        other = lax.rem(part + 1 + lax.rem(step, parts), parts)
         there = jnp.where(step < parts - 1, section, 1 - section)
+        other = jnp.where(step < parts - 1, other, lax.rem(part + step, parts))
         pl.semaphore_signal(
             barrier, inc=1, device_id=(there, replica, other), device_id_type=MESH
         )
 
-    loop(count, greet_column)
-    loop(2 * (parts - 1), greet_row)
+    loop(replicas - 1, greet_column)
+    loop(2 * parts - 1, greet_row)
 
     rows_of = 2 * batches
     row_index = lax.rem(iota((rows_of, tokens), 0), batches)
@@ -226,8 +232,8 @@
             seen = jnp.max(jnp.where(same, 1.0, 0.0), axis=0, keepdims=True)
             first[index, :] = 1.0 - seen
 
-    loop(replicas // 4, find_first)
-    pl.semaphore_wait(barrier, count - 1 + 2 * (parts - 1))
+    loop(count // 4, find_first)
+    pl.semaphore_wait(barrier, replicas - 1 + 2 * parts - 1)
 
     def weight_source(target):
         features = pl.ds(pl.multiple_of(target * width, width), width)
@@ -329,43 +335,61 @@
     def shard_of(rows):
         return jnp.floor(rows * (1.0 / vocab_rows))
 
+    def chip_of(rows):
+        shards = shard_of(rows)
+        return shards - replicas * jnp.floor(shards * (1.0 / replicas))
+
     triangle = jnp.where(earlier, 1.0, 0.0).astype(BF)
     me_f = me.astype(F32)
-    group = min(replicas, max(1, 2 * tokens // per_pair))
+    here_f = replica.astype(F32)
+    group = min(replicas, max(1, 2 * tokens // half))
 
     def row_copy(step):
         other, device = column_peer(step)
-        return remote(send.at[other], recv.at[me], row_send.at[step], row_recv.at[me], device)
-
-    def send_rows(half):
-        half_rows = pl.ds(half * replicas, replicas)
-        mine = jnp.where(shard_of(ids_ref[half_rows, :]) == me_f, first[half_rows, :], 0.0)
-        rank[...] = jnp.where(mine > 0.0, dot(mine.astype(BF), triangle), -1.0)
-
-        def find_lid(step):
-            for inner in range(4):
-                index = step * 4 + inner
-                there = half * replicas + index
-                row = ids_ref[pl.ds(there, 1), :] - (me_f * vocab_rows - 1.0)
-                picks = rank[pl.ds(index, 1), :].astype(jnp.int32) == iota(
+        return remote(
+            send.at[other],
+            recv.at[section, replica],
+            row_send.at[step],
+            row_recv.at[replica],
+            device,
+        )
+
+    def ranks(first_row):
+        rows = pl.ds(first_row, replicas)
+        mine = jnp.where(chip_of(ids_ref[rows, :]) == here_f, first[rows, :], 0.0)
+        return mine, dot(mine.astype(BF), triangle)
+
+    mine, order = ranks(0)
+    before = total(mine)
+    rank[pl.ds(0, replicas), :] = jnp.where(mine > 0.0, order, -1.0)
+    mine, order = ranks(replicas)
+    rank[pl.ds(replicas, replicas), :] = jnp.where(mine > 0.0, order + before, -1.0)
+
+    def find_lid(step):
+        for inner in range(2):
+            index = step * 2 + inner
+            found = jnp.zeros((per_pair, 1), F32)
+            for offset in (0, replicas):
+                row = ids_ref[pl.ds(index + offset, 1), :] - (me_f * vocab_rows - 1.0)
+                picks = rank[pl.ds(index + offset, 1), :].astype(jnp.int32) == iota(
                     (per_pair, tokens), 0
                 )
-                found = total(jnp.where(picks, jnp.broadcast_to(row, picks.shape), 0.0))
-                lid[pl.ds(pl.multiple_of(there * per_pair, per_pair), per_pair), :] = (
-                    jnp.broadcast_to(found - 1.0, (per_pair, tokens)).astype(jnp.int32)
-                )
-
-        loop(replicas // 4, find_lid)
-
+                found += total(jnp.where(picks, jnp.broadcast_to(row, picks.shape), 0.0))
+            whole = jnp.broadcast_to(found - 1.0, (per_pair, tokens)).astype(jnp.int32)
+            for side in range(2):
+                place = pl.multiple_of((side * replicas + index) * half, half)
+                lid[pl.ds(place, half), :] = whole[side * half : (side + 1) * half]
+
+    loop(replicas // 2, find_lid)
+
+    def pick_rows(side, put):
         def chunk(block):
-            base = half * replicas + block * group
+            base = block * group
 
             def mark(step):
-                other = column_peer(base + step)[0]
-                wanted = lid[
-                    pl.ds(pl.multiple_of(other * per_pair, per_pair), per_pair), :
-                ]
-                there = pl.ds(pl.multiple_of(step * per_pair, per_pair), per_pair)
+                place = pl.multiple_of((side * replicas + base + step) * half, half)
+                wanted = lid[pl.ds(place, half), :]
+                there = pl.ds(pl.multiple_of(step * half, half), half)
                 for lane in range(vocab_rows // tokens):
                     hit = wanted == iota(wanted.shape, 1) + lane * tokens
                     onehot[there, pl.ds(lane * tokens, tokens)] = jnp.where(
@@ -374,41 +398,47 @@
 
             loop(group, mark)
             found = dot(onehot[...], table[...]).astype(BF)
-            for step in range(group):
-                other = column_peer(base + step)[0]
-                send[other] = found[step * per_pair : (step + 1) * per_pair]
-
-            def go(step):
-                @pl.when(column_peer(base + step)[0] != me)
-                def _():
-                    row_copy(base + step).start()
-
-            loop(group, go)
+            put(pl.ds(base, group), found.reshape(group, half, width))
 
         if group == replicas:
             chunk(0)
         else:
             loop(replicas // group, chunk)
 
+    def swap_copy(turn):
+        return remote(
+            swap_out, swap_in, swap_send.at[turn], swap_recv.at[turn], partner
+        )
+
+    def put_swap(place, values):
+        swap_out[place] = values
+
+    def put_send(place, values):
+        send[place] = values
+
     load.wait()
-    send_rows(0)
-    loop(replicas // 4, lambda step: find_first(step + replicas // 4))
-    send_rows(1)
-    recv[me] = send[me]
+    pick_rows(1 - section, put_swap)
+    swap_copy(0).start()
+    pick_rows(section, put_send)
+    swap_copy(0).wait()
+    send[...] = send[...] + swap_in[...]
+    loop(replicas - 1, lambda step: row_copy(step).start())
+    recv[section, replica] = send[replica]
 
     @pl.when(section == 0)
     def _():
-        relay_on((0, 1))
-
-    shard = shard_of(ids_ref[...])
+        relay_on((0, 1, 2))
+
+    chip = chip_of(ids_ref[...])
 
     def fill(step, most):
         for inner in range(4):
-            held = jnp.where(shard == (step * 4 + inner).astype(F32), first[...], 0.0)
-            most = jnp.maximum(most, total(held))
+            held = jnp.where(chip == (step * 4 + inner).astype(F32), first[...], 0.0)
+            held = total(held)
+            most = jnp.maximum(most, held[:replicas] + held[replicas:])
         return most
 
-    most = lax.fori_loop(0, count // 4, fill, jnp.zeros((count, 1), F32))
+    most = lax.fori_loop(0, replicas // 4, fill, jnp.zeros((replicas, 1), F32))
     over_ref[...] = jnp.broadcast_to(jnp.max(most, axis=0, keepdims=True), over_ref.shape)
     eye = iota((tokens, tokens), 0) == iota((tokens, tokens), 1)
 
@@ -421,175 +451,53 @@
     own_row = ids_ref[pl.ds(me, 1), :]
     own_first = first[pl.ds(me, 1), :]
     own_column = to_column(own_row)
-    shard_row = shard_of(own_row)
-    counted = (shard_of(own_column) == shard_row) & earlier & (to_column(own_first) > 0.0)
-    slot_row = shard_row * per_pair + jnp.sum(
-        jnp.where(counted, 1.0, 0.0), axis=0, keepdims=True
+    chip_row = chip_of(own_row)
+    counted = (chip_of(own_column) == chip_row) & earlier & (to_column(own_first) > 0.0)
+    main_chip = chip_of(to_column(ids_ref[pl.ds(replica, 1), :]))
+    main_first = to_column(first[pl.ds(replica, 1), :])
+    ahead = jnp.where((main_chip == chip_row) & (main_first > 0.0), 1.0, 0.0)
+    rank_row = jnp.sum(
+        jnp.where(counted, 1.0, 0.0) + ahead * section.astype(F32), axis=0, keepdims=True
     )
+    side_row = jnp.floor(rank_row * (1.0 / half))
+    slot_row = (side_row * (replicas - 1) + chip_row) * half + rank_row
     leads = (own_column == own_row) & (own_first > 0.0)
     slot_column = total(jnp.where(leads, jnp.broadcast_to(slot_row, leads.shape), 0.0))
 
-    def row_wait(step):
-        other, device = column_peer(step)
-
-        @pl.when(other != me)
-        def _():
+    def pass_copy(whole, turn, block):
+        return remote(
+            whole.at[section, block],
+            whole.at[section, block],
+            pass_send.at[turn, block],
+            pass_recv.at[turn, block],
+            partner,
+        )
+
+    def collect(whole, turn, send_sem, recv_sem):
+        pass_copy(whole, turn, replica).start()
+
+        def arrive(step):
+            other = lax.rem(replica + replicas - 1 - step, replicas)
             remote(
-                send.at[me], recv.at[other], row_send.at[step], row_recv.at[other], device
+                whole.at[section, other],
+                whole.at[section, other],
+                send_sem.at[step],
+                recv_sem.at[other],
+                partner,
             ).wait_recv()
-
-    loop(count, row_wait)
-    slot_of = slot_column.astype(jnp.int32)
-    spread = jnp.where(slot_of == iota((tokens, slots), 1), 1.0, 0.0).astype(BF)
-    rows_ref[...] = dot(spread, recv[...].reshape(slots, width)).astype(BF)
-
-    features = pl.ds(pl.multiple_of(part * width, width), width)
-    gain = gain_ref[0:1, features]
-    gain_main = mtp_gain_ref[0:1, features]
-    gain_next = mtp_gain_ref[1:2, features]
-
-    def inverse(sum_of_squares):
-        return lax.rsqrt(sum_of_squares / model_width + EPS)
-
-    def lanes(index, size):
-        return pl.ds(pl.multiple_of(index * size, size), size)
-
-    def put_stats(slot, columns):
-        rows = [to_row(column) for column in columns]
-        rows = rows + [jnp.zeros_like(rows[0])] * (8 - len(rows))
-        stat_in[slot, part] = jnp.concatenate(rows, axis=0)
-
-    def get_stats(slot, number):
-        value = stat_in[slot, 0]
-        for index in range(1, parts):
-            value = value + stat_in[slot, index]
-        return [to_column(value[index : index + 1, :]) for index in range(number)]
-
-    def stat_copy(slot, step):
-        return remote(
-            stat_in.at[slot, part],
-            stat_in.at[slot, part],
-            stat_send.at[slot, step],
-            stat_recv.at[slot, part],
-            row_peer(step)[1],
-        )
-
-    def share_stats(slot):
-        loop(parts - 1, lambda step: stat_copy(slot, step).start())
-
-    def wait_stats(slot):
-        def one(step):
-            other, device = row_peer(step)
+            pass_copy(whole, turn, other).start()
+
+        def passed(block):
             remote(
-                stat_in.at[slot, other],
-                stat_in.at[slot, other],
-                stat_send.at[slot, step],
-                stat_recv.at[slot, other],
-                device,
+                whole.at[1 - section, block],
+                whole.at[1 - section, block],
+                pass_send.at[turn, block],
+                pass_recv.at[turn, block],
+                partner,
             ).wait()
 
-        loop(parts - 1, one)
-
-    def tell_copy(step):
-        other = lax.rem(part + step, parts)
-        return remote(
-            stat_in.at[1, part],
-            stat_in.at[1, part],
-            stat_send.at[1, step],
-            stat_recv.at[1, part],
-            (1 - section, replica, other),
-        )
-
-    def gate_up_start(normed):
-        def partial(other):
-            part_out[other] = dot(normed, gu[other]).astype(BF)
-
-        def one(step):
-            other, device = row_peer(step)
-            weight_wait(0, step)
-            weight_wait(1, step)
-            partial(other)
-            remote(
-                part_out.at[other],
-                part_in.at[part],
-                part_send.at[step],
-                part_recv.at[part],
-                device,
-            ).start()
-
-        loop(parts - 1, one)
-        own_weight(0).wait()
-        own_weight(1).wait()
-        partial(part)
-
-    def gate_up_wait():
-        def one(step, value):
-            other, device = row_peer(step)
-            remote(
-                part_in.at[other],
-                part_in.at[other],
-                part_send.at[step],
-                part_recv.at[other],
-                device,
-            ).wait()
-            return value + part_in[other].astype(F32)
-
-        return lax.fori_loop(0, parts - 1, one, part_out[part].astype(F32))
-
-    def down_wait():
-        loop(parts - 1, lambda step: weight_wait(2, step))
-        own_weight(2).wait()
-
-    def grad_hidden_start(grad):
-        early_out[...] = dot_t(grad, down[...].reshape(parts * hidden, width)).astype(BF)
-
-        def one(step):
-            other, device = row_peer(step)
-            remote(
-                early_out.at[:, lanes(other, hidden)],
-                early_in.at[part],
-                early_send.at[step],
-                early_recv.at[part],
-                device,
-            ).start()
-
-        loop(parts - 1, one)
-
-    def grad_hidden_wait():
-        def one(step, value):
-            other, device = row_peer(step)
-            remote(
-                early_in.at[other],
-                early_in.at[other],
-                early_send.at[step],
-                early_recv.at[other],
-                device,
-            ).wait()
-            return value + early_in[other].astype(F32)
-
-        return lax.fori_loop(
-            0, parts - 1, one, early_out[:, lanes(part, hidden)].astype(F32)
-        )
-
-    def share_columns(whole, size, send_sem, recv_sem):
-        def start(step):
-            device = row_peer(step)[1]
-            own = whole.at[:, lanes(part, size)]
-            remote(own, own, send_sem.at[step], recv_sem.at[part], device).start()
-
-        def wait(step):
-            other, device = row_peer(step)
-            theirs = whole.at[:, lanes(other, size)]
-            remote(theirs, theirs, send_sem.at[step], recv_sem.at[other], device).wait()
-
-        loop(parts - 1, start)
-        loop(parts - 1, wait)
-
-    def slopes(gate, up, grad_hidden):
-        sigmoid = jax.nn.sigmoid(gate)
-        grad_gate = grad_hidden * up * sigmoid * (1.0 + gate * (1.0 - sigmoid))
-        grad_up = grad_hidden * gate * sigmoid
-        return jnp.concatenate([grad_gate, grad_up], axis=1).astype(BF)
+        loop(replicas - 1, arrive)
+        loop(replicas, passed)
 
     def block_copy(whole, send_sem, recv_sem, block, step, device):
         return remote(
@@ -635,6 +543,159 @@
         for other in held[1:]:
             value = value + other
         return value
+
+    collect(recv, 0, row_send, row_recv)
+    slot_of = slot_column.astype(jnp.int32)
+    spread = jnp.where(slot_of == iota((tokens, slots), 1), 1.0, 0.0).astype(BF)
+    rows_ref[...] = dot(spread, recv[...].reshape(slots, width)).astype(BF)
+
+    features = pl.ds(pl.multiple_of(part * width, width), width)
+    gain = gain_ref[0:1, features]
+    gain_main = mtp_gain_ref[0:1, features]
+    gain_next = mtp_gain_ref[1:2, features]
+
+    def inverse(sum_of_squares):
+        return lax.rsqrt(sum_of_squares / model_width + EPS)
+
+    def lanes(index, size):
+        return pl.ds(pl.multiple_of(index * size, size), size)
+
+    def put_stats(slot, columns):
+        rows = [to_row(column) for column in columns]
+        rows = rows + [jnp.zeros_like(rows[0])] * (8 - len(rows))
+        stat_in[slot, part] = jnp.concatenate(rows, axis=0)
+
+    def get_stats(slot, number):
+        value = stat_in[slot, 0]
+        for index in range(1, parts):
+            value = value + stat_in[slot, index]
+        return [to_column(value[index : index + 1, :]) for index in range(number)]
+
+    def stat_copy(slot, step):
+        return remote(
+            stat_in.at[slot, part],
+            stat_in.at[slot, part],
+            stat_send.at[slot, step],
+            stat_recv.at[slot, part],
+            row_peer(step)[1],
+        )
+
+    def share_stats(slot):
+        loop(parts - 1, lambda step: stat_copy(slot, step).start())
+
+    def wait_stats(slot):
+        def one(step):
+            other, device = row_peer(step)
+            remote(
+                stat_in.at[slot, other],
+                stat_in.at[slot, other],
+                stat_send.at[slot, step],
+                stat_recv.at[slot, other],
+                device,
+            ).wait()
+
+        loop(parts - 1, one)
+
+    def tell_copy(step):
+        other = lax.rem(part + step, parts)
+        return remote(
+            stat_in.at[1, part],
+            stat_in.at[1, part],
+            stat_send.at[1, step],
+            stat_recv.at[1, part],
+            (1 - section, replica, other),
+        )
+
+    def gate_up_start(normed):
+        def partial(other):
+            part_out[other] = dot(normed, gu[other]).astype(BF)
+
+        def one(step):
+            other, device = row_peer(step)
+            weight_wait(0, step)
+            weight_wait(1, step)
+            partial(other)
+            remote(
+                part_out.at[other],
+                part_in.at[part],
+                part_send.at[step],
+                part_recv.at[part],
+                device,
+            ).start()
+
+        loop(parts - 1, one)
+        own_weight(0).wait()
+        own_weight(1).wait()
+        partial(part)
+
+    def gate_up_wait():
+        def one(step, value):
+            other, device = row_peer(step)
+            remote(
+                part_in.at[other],
+                part_in.at[other],
+                part_send.at[step],
+                part_recv.at[other],
+                device,
+            ).wait()
+            return value + part_in[other].astype(F32)
+
+        return lax.fori_loop(0, parts - 1, one, part_out[part].astype(F32))
+
+    def down_wait():
+        loop(parts - 1, lambda step: weight_wait(2, step))
+        own_weight(2).wait()
+
+    def grad_hidden_start(grad):
+        early_out[...] = dot_t(grad, down[...].reshape(parts * hidden, width)).astype(BF)
+
+        def one(step):
+            other, device = row_peer(step)
+            remote(
+                early_out.at[:, lanes(other, hidden)],
+                early_in.at[part],
+                early_send.at[step],
+                early_recv.at[part],
+                device,
+            ).start()
+
+        loop(parts - 1, one)
+
+    def grad_hidden_wait():
+        def one(step, value):
+            other, device = row_peer(step)
+            remote(
+                early_in.at[other],
+                early_in.at[other],
+                early_send.at[step],
+                early_recv.at[other],
+                device,
+            ).wait()
+            return value + early_in[other].astype(F32)
+
+        return lax.fori_loop(
+            0, parts - 1, one, early_out[:, lanes(part, hidden)].astype(F32)
+        )
+
+    def share_columns(whole, size, send_sem, recv_sem):
+        def start(step):
+            device = row_peer(step)[1]
+            own = whole.at[:, lanes(part, size)]
+            remote(own, own, send_sem.at[step], recv_sem.at[part], device).start()
+
+        def wait(step):
+            other, device = row_peer(step)
+            theirs = whole.at[:, lanes(other, size)]
+            remote(theirs, theirs, send_sem.at[step], recv_sem.at[other], device).wait()
+
+        loop(parts - 1, start)
+        loop(parts - 1, wait)
+
+    def slopes(gate, up, grad_hidden):
+        sigmoid = jax.nn.sigmoid(gate)
+        grad_gate = grad_hidden * up * sigmoid * (1.0 + gate * (1.0 - sigmoid))
+        grad_up = grad_hidden * gate * sigmoid
+        return jnp.concatenate([grad_gate, grad_up], axis=1).astype(BF)
 
     def return_blocks(terms):
         up_one = (section, replica, away(1, 0))
@@ -707,7 +768,6 @@
         put_stats(0, [total(rows * rows)])
         share_stats(0)
         gate_up_start((rows * gain).astype(BF))
-        relay_on((2,))
         wait_stats(0)
         scale = inverse(get_stats(0, 1)[0])
         whole = gate_up_wait() * scale
@@ -732,6 +792,8 @@
         wide_in[:, lanes(part, 2 * hidden)] = slopes(
             whole[:, :hidden], whole[:, hidden:], grad_hidden
         )
+        put_stats(2, [total(wide_in[:, lanes(part, 2 * hidden)].astype(F32) * whole)])
+        share_stats(2)
         share_columns(wide_in, 2 * hidden, wide_send, wide_recv)
         scaled = dot_t(wide_in[:, pl.ds(0, 2 * hidden)], gu[0])
         for index in range(1, parts):
@@ -740,12 +802,10 @@
             )
         scaled = scaled * gain
         rows = rows_ref[...].astype(F32)
-        put_stats(2, [total(rows * scaled)])
-        share_stats(2)
         wait_stats(2)
         mean = get_stats(2, 1)[0] / model_width
         scale = inverse(get_stats(0, 1)[0])
-        result = grad.astype(F32) + scale * scaled - rows * (scale * scale * scale * mean)
+        result = grad.astype(F32) + scale * scaled - rows * (scale * scale * mean)
         grad_ref[...] = result.astype(BF)
 
     @pl.when(section == 1)
@@ -821,35 +881,39 @@
         grad_ref[...] = grad_next.astype(BF)
         over.wait_send()
 
-    def row_done(step):
-        @pl.when(column_peer(step)[0] != me)
-        def _():
-            row_copy(step).wait_send()
-
-    loop(count, row_done)
+    loop(replicas - 1, lambda step: row_copy(step).wait_send())
     slot_back = to_row(slot_column).astype(jnp.int32)
-    group_rows = group * per_pair
-
-    def pack(block):
-        hit = slot_back == iota((group_rows, tokens), 0) + block * group_rows
-        found = dot(jnp.where(hit, 1.0, 0.0).astype(BF), grad_ref[...]).astype(BF)
-        send[pl.ds(block * group, group)] = found.reshape(group, per_pair, width)
-
-    loop(count // group, pack)
+    group_rows = group * half
+
+    def pack_rows(side, put):
+        def pack(block):
+            base = (side * (replicas // group) + block) * group_rows
+            hit = slot_back == iota((group_rows, tokens), 0) + base
+            found = dot(jnp.where(hit, 1.0, 0.0).astype(BF), grad_ref[...]).astype(BF)
+            put(pl.ds(block * group, group), found.reshape(group, half, width))
+
+        if group == replicas:
+            pack(0)
+        else:
+            loop(replicas // group, pack)
 
     def sum_copy(step):
         other, device = column_peer(step)
         return remote(
-            send.at[other], sums_ref.at[me], sum_send.at[step], sum_recv.at[me], device
-        )
-
-    def sum_start(step):
-        @pl.when(column_peer(step)[0] != me)
-        def _():
-            sum_copy(step).start()
-
-    loop(count, sum_start)
-    sums_ref[me] = send[me]
+            send.at[other],
+            sums_ref.at[section, replica],
+            sum_send.at[step],
+            sum_recv.at[replica],
+            device,
+        )
+
+    pack_rows(1 - section, put_swap)
+    swap_copy(1).start()
+    pack_rows(section, put_send)
+    swap_copy(1).wait()
+    send[...] = send[...] + swap_in[...]
+    loop(replicas - 1, lambda step: sum_copy(step).start())
+    sums_ref[section, replica] = send[replica]
 
     @pl.when(section == 0)
     def _():
@@ -859,20 +923,8 @@
                 forward_copy(kind, way).wait_send()
             loop(parts - 3, lambda step: direct_copy(kind, step).wait_send())
 
-    def sum_wait(step):
-        other, device = column_peer(step)
-
-        @pl.when(other != me)
-        def _():
-            remote(
-                send.at[other],
-                sums_ref.at[other],
-                sum_send.at[step],
-                sum_recv.at[other],
-                device,
-            ).wait()
-
-    loop(count, sum_wait)
+    collect(sums_ref, 1, sum_send, sum_recv)
+    loop(replicas - 1, lambda step: sum_copy(step).wait_send())
 
 
 def place_kernel(lid_ref, sums_ref, out_ref):
@@ -916,14 +968,15 @@
     tokens = batches * (token_ids.shape[1] // replicas)
     vocab_rows, width = embed_table.shape
     hidden = w_gate.shape[2]
-    slots = count * per_pair
-    picked = min(replicas * per_pair, max(2 * tokens, per_pair))
+    half = per_pair // 2
+    slots = replicas * per_pair
+    picked = min(replicas * half, max(2 * tokens, half))
     block = pltpu.VMEM((parts, tokens, width), BF)
     one = pltpu.SemaphoreType.DMA
     return pl.pallas_call(
         functools.partial(step_kernel, sections, replicas, parts, per_pair),
         out_shape=(
-            jax.ShapeDtypeStruct((count, per_pair, width), BF),
+            jax.ShapeDtypeStruct((2, replicas, half, width), BF),
             jax.ShapeDtypeStruct((8, slots), jnp.int32),
             jax.ShapeDtypeStruct((8, 128), F32),
         ),
@@ -933,11 +986,13 @@
             pltpu.VMEM((vocab_rows, width), BF),
             pltpu.VMEM((count, tokens), F32),
             pltpu.VMEM((count, tokens), F32),
-            pltpu.VMEM((replicas, tokens), F32),
+            pltpu.VMEM((count, tokens), F32),
             pltpu.VMEM((slots, tokens), jnp.int32),
             pltpu.VMEM((picked, vocab_rows), BF),
-            pltpu.VMEM((count, per_pair, width), BF),
-            pltpu.VMEM((count, per_pair, width), BF),
+            pltpu.VMEM((replicas, half, width), BF),
+            pltpu.VMEM((replicas, half, width), BF),
+            pltpu.VMEM((replicas, half, width), BF),
+            pltpu.VMEM((2, replicas, half, width), BF),
             pltpu.VMEM((tokens, width), BF),
             pltpu.VMEM((tokens, width), BF),
             pltpu.VMEM((parts, width, 2 * hidden), BF),
@@ -960,10 +1015,14 @@
             pltpu.VMEM((tokens, 2 * hidden), F32),
             one,
             one,
-            dma(count),
-            dma(count),
-            dma(count),
-            dma(count),
+            dma(2),
+            dma(2),
+            dma(replicas),
+            dma(replicas),
+            dma(replicas),
+            dma(replicas),
+            dma(2, replicas),
+            dma(2, replicas),
             dma(3),
             dma(3, parts),
             dma(3, parts),
@@ -1016,7 +1075,7 @@
 
 def body(*arguments):
     vocab_rows = arguments[2].shape[0]
-    positions = arguments[0].shape[0] * (arguments[0].shape[1] // lax.axis_size("dp"))
+    positions = 2 * arguments[0].shape[0] * (arguments[0].shape[1] // lax.axis_size("dp"))
     sums, lid_row, most = train_step(FEW_SLOTS, *arguments)
 
     def few(sums, lid_row, *given):

time: 153 us -> 144 us (0.941)
  Pallas kernels: 149 us -> 140 us
    pallas_call x1, Pallas kernels: 144 us -> 135 us  [train_step(): pl.pallas_call(functools.partial(step_kernel, sections, replicas, parts,...]
where the time goes in v4:
time: 144 us; the launch traced here: 143 us
  Pallas kernels  140 us (97%)
  local copies, waits for them, and re-layouts  3.04 us (2%)
    pallas_call x1, Pallas kernels, train_step(): pl.pallas_call(functools.partial(step_kernel, sections, replicas, parts,...  135 us
    pallas_call x1, Pallas kernels, place(): pl.pallas_call(place_kernel, grid=(vocab_rows // block,), out_shape=jax.S...  4.79 us

profile of v4, /device:TPU:1, one launch (start us, length us, event | category | flops | bytes accessed | tf_op | source)
XLA Modules:
  0.0 143.4 jit_solution(4081659010507173794)
XLA Ops:
  0.0 0.0 copy-start
  0.0 0.0 copy-start.2
  0.0 0.0 copy-start.3
  0.0 134.9 %train_step_32.1 = (bf16[2,16,16,896]{3,2,1,0:T(8,128)(2,1)}, s32[8,512]{1,0:T(8,128)}, f32[8,128]{1,0:T(8,128)}) custom-call(s32[4,512]{1,0:T(4,128)} %token_ids_ref.1, s32[4,512]{1,0:T(4,128)} %next_ids_ref.1, bf16[128,896]{1,0:T(8,128)(2,1)} %bitcast.21, bf16[128,896]{1,0:T(8,128)(2,1)} %bitcast.23, f32[1,7168]{1,0:T(1,128)} %gain_ref.1, ...), custom_call_target="tpu_custom_call" | custom-call | tf_op jit(solution)/shard_map/train_step_32/pallas_call | solution.py:976
  134.9 1.2 slice.3
  136.7 0.0 copy-done
  136.7 0.0 copy-done.2
  136.7 0.0 copy-done.3
  136.7 4.8 %conditional.1 = (bf16[2048,896]{1,0:T(8,128)(2,1)S(1)}) conditional(s32[]{:T(128)} %bitcast.12, (bf16[4,32,896]{2,1,0:T(8,128)(2,1)S(1)}, bf16[4,32,896]{2,1,0:T(8,128)(2,1)S(1)}, bf16[1,7168,128]{2,1,0:T(8,128)(2,1)}, bf16[1,7168,128]{2,1,0:T(8,128)(2,1)}, bf16[1,128,7168]{2,1,0:T(8,128)(2,1)}, /*index=5*/s32[4,512]{1,0:T(4,128)}, ...), branch_computations={%region_0.0_spmd, %region_1.0_spmd} | conditional | bytes 8 | solution.py:1088
  136.8 4.8 %place_rows.3 = bf16[2048,896]{1,0:T(8,128)(2,1)S(1)} custom-call(s32[8,512]{1,0:T(8,128)} %get-tuple-element.44.lid_ref, bf16[512,896]{1,0:T(8,128)(2,1)} %bitcast.20), custom_call_target="tpu_custom_call" | custom-call | tf_op jit(solution)/shard_map/cond/branch_1_fun/place_rows/pallas_call | solution.py:1062
  141.6 0.0 copy-start.1
  141.6 1.8 %copy-done.1 = bf16[2048,896]{1,0:T(8,128)(2,1)} copy-done((bf16[2048,896]{1,0:T(8,128)(2,1)}, bf16[2048,896]{1,0:T(8,128)(2,1)S(1)}, u32[]{:S(2)}) %copy-start.1) | copy-done | bytes 3670040
Async XLA Ops:
  0.0 136.7 %copy-start = (bf16[2048,896]{1,0:T(8,128)(2,1)S(1)}, bf16[2048,896]{1,0:T(8,128)(2,1)}, u32[]{:S(2)}) copy-start(bf16[2048,896]{1,0:T(8,128)(2,1)} %table_hbm.1) | copy-start | bytes 11010052
  0.0 136.7 %copy-start.2 = (bf16[4,32,896]{2,1,0:T(8,128)(2,1)S(1)}, bf16[4,32,896]{2,1,0:T(8,128)(2,1)}, u32[]{:S(2)}) copy-start(bf16[4,32,896]{2,1,0:T(8,128)(2,1)} %param.20) | copy-start | bytes 688132
  0.0 136.7 %copy-start.3 = (bf16[4,32,896]{2,1,0:T(8,128)(2,1)S(1)}, bf16[4,32,896]{2,1,0:T(8,128)(2,1)}, u32[]{:S(2)}) copy-start(bf16[4,32,896]{2,1,0:T(8,128)(2,1)} %param.21) | copy-start | bytes 688132
  141.6 1.8 %copy-start.1 = (bf16[2048,896]{1,0:T(8,128)(2,1)}, bf16[2048,896]{1,0:T(8,128)(2,1)S(1)}, u32[]{:S(2)}) copy-start(bf16[2048,896]{1,0:T(8,128)(2,1)S(1)} %get-tuple-element.55) | copy-start | bytes 11010052

commit v5 on v4

--- a/solution.py
+++ b/solution.py
@@ -128,6 +128,7 @@
     weight_recv,
     relay_send,
     relay_recv,
+    across_send,
     part_send,
     part_recv,
     early_send,
@@ -146,7 +147,6 @@
     cot_recv,
     back_send,
     back_recv,
-    back_relay_send,
     back_relay_recv,
 ):
     section = lax.axis_index("section")
@@ -300,11 +300,24 @@
 
         loop(parts, one)
 
+    level = lax.rem(replica // 2, 2)
+    across = (section, replica + 2 - 4 * level, part)
+
+    def by_level(then, swap=0):
+        for value in range(2):
+
+            @pl.when(level == value)
+            def _():
+                then(value if swap == 0 else 1 - value)
+
+    def weights_begin(kind):
+        for way in range(2):
+            relay_copy(kind, way).start()
+        loop(parts - 3, lambda step: direct_copy(kind, step).start())
+
     def weights_start():
-        for kind in range(3):
-            for way in range(2):
-                relay_copy(kind, way).start()
-            loop(parts - 3, lambda step: direct_copy(kind, step).start())
+        by_level(weights_begin)
+        weights_begin(2)
         for kind in range(3):
             own_weight(kind).start()
 
@@ -323,6 +336,29 @@
             weight_recv.at[kind, other],
             device,
         ).wait_recv()
+
+    def across_copy(kind, step):
+        other = row_peer(step)[0]
+        slot = weight_slot(other)[kind]
+        return remote(
+            slot, slot, across_send.at[step], weight_recv.at[kind, other], across
+        )
+
+    def hand_across(kind):
+        def one(step):
+            weight_wait(kind, step)
+            across_copy(kind, step).start()
+
+        loop(parts - 1, one)
+
+    def weights_done(kind):
+        for way in range(2):
+            relay_copy(kind, way).wait_send()
+            forward_copy(kind, way).wait_send()
+        loop(parts - 3, lambda step: direct_copy(kind, step).wait_send())
+
+    def across_done(kind):
+        loop(parts - 1, lambda step: across_copy(kind, step).wait_send())
 
     @pl.when(section == 0)
     def _():
@@ -427,7 +463,9 @@
 
     @pl.when(section == 0)
     def _():
-        relay_on((0, 1, 2))
+        by_level(lambda kind: relay_on((kind,)))
+        by_level(hand_across)
+        relay_on((2,))
 
     chip = chip_of(ids_ref[...])
 
@@ -612,8 +650,7 @@
 
         def one(step):
             other, device = row_peer(step)
-            weight_wait(0, step)
-            weight_wait(1, step)
+            by_level(lambda kind: weight_wait(kind, step), swap=1)
             partial(other)
             remote(
                 part_out.at[other],
@@ -700,51 +737,37 @@
     def return_blocks(terms):
         up_one = (section, replica, away(1, 0))
         down_one = (section, replica, away(ring - 1, 0))
-        plan = [
-            (away(2, 0), up_one, 0),
-            (away(2, 1), down_one, 1),
-            (away(1, 1), None, None),
-            (away(ring - 1, 1), None, None),
-            (away(1, 0), None, None),
-            (away(ring - 1, 0), None, None),
-            (away(0, 1), None, None),
-        ]
         sent = []
-        for step, (block, device, way) in enumerate(plan):
-            back_out[block] = dot_t(terms, gu[block]).astype(BF)
-            target = back_in.at[part] if way is None else back_relay.at[way]
-            arrived = back_recv.at[part] if way is None else back_relay_recv.at[way]
+
+        def go(block, values, target, arrived, device):
+            back_out[block] = values.astype(BF)
             copy = remote(
-                back_out.at[block],
-                target,
-                back_send.at[step],
-                arrived,
-                (section, replica, block) if device is None else device,
+                back_out.at[block], target, back_send.at[len(sent)], arrived, device
             )
             copy.start()
             sent.append(copy)
+
+        for way, device in enumerate((up_one, down_one)):
+            block = away(2, way)
+            values = dot_t(terms, gu[block])
+            go(block, values, back_relay.at[way], back_relay_recv.at[way], device)
+        for block in (away(1, 1), away(ring - 1, 0), away(0, 1)):
+            values = dot_t(terms, gu[block])
+            device = (section, replica, block)
+            go(block, values, back_in.at[part], back_recv.at[part], device)
+        for way, block in enumerate((away(1, 0), away(ring - 1, 1))):
+            values = dot_t(terms, gu[block])
+            sent[way].wait_recv()
+            device = (section, replica, block)
+            values = values + back_relay[way].astype(F32)
+            go(block, values, back_in.at[part], back_recv.at[part], device)
         own = dot_t(terms, gu[part])
-        for way in range(2):
-            origin = away(ring - 1 - way * (ring - 2), 0)
-            final = away(1 + way * (ring - 2), way)
-            sent[way].wait_recv()
-            copy = remote(
-                back_relay.at[way],
-                back_in.at[origin],
-                back_relay_send.at[way],
-                back_recv.at[origin],
-                (section, replica, final),
-            )
-            copy.start()
-            sent.append(copy)
         for block in (
             away(0, 1),
             away(1, 0),
+            away(ring - 1, 1),
             away(ring - 1, 0),
             away(1, 1),
-            away(ring - 1, 1),
-            away(2, 0),
-            away(2, 1),
         ):
             remote(
                 back_in.at[block],
@@ -917,11 +940,9 @@
 
     @pl.when(section == 0)
     def _():
-        for kind in range(3):
-            for way in range(2):
-                relay_copy(kind, way).wait_send()
-                forward_copy(kind, way).wait_send()
-            loop(parts - 3, lambda step: direct_copy(kind, step).wait_send())
+        by_level(weights_done)
+        by_level(across_done)
+        weights_done(2)
 
     collect(sums_ref, 1, sum_send, sum_recv)
     loop(replicas - 1, lambda step: sum_copy(step).wait_send())
@@ -1029,12 +1050,13 @@
             dma(3, parts),
             dma(3, 2),
             dma(3, 2),
+            dma(parts),
         ]
         + [dma(parts)] * 8
         + [dma(4, parts)] * 2
         + [one] * 2
         + [dma(parts)] * 6
-        + [dma(2)] * 2,
+        + [dma(2)],
         compiler_params=pltpu.CompilerParams(
             collective_id=0 if per_pair == FEW_SLOTS else 1,
             has_side_effects=True,

time: 144 us -> 138 us (0.958)
  Pallas kernels: 140 us -> 134 us
    pallas_call x1, Pallas kernels: 135 us -> 129 us  [train_step(): pl.pallas_call(functools.partial(step_kernel, sections, replicas, parts,...]
where the time goes in v5:
time: 138 us; the launch traced here: 137 us
  Pallas kernels  134 us (97%)
  local copies, waits for them, and re-layouts  3.04 us (2%)
    pallas_call x1, Pallas kernels, train_step(): pl.pallas_call(functools.partial(step_kernel, sections, replicas, parts,...  129 us
    pallas_call x1, Pallas kernels, place(): pl.pallas_call(place_kernel, grid=(vocab_rows // block,), out_shape=jax.S...  4.79 us

profile of v5, /device:TPU:1, one launch (start us, length us, event | category | flops | bytes accessed | tf_op | source)
XLA Modules:
  0.0 137.3 jit_solution(18132672418619967339)
XLA Ops:
  0.0 0.0 copy-start
  0.0 0.0 copy-start.2
  0.0 0.0 copy-start.3
  0.0 128.8 %train_step_32.1 = (bf16[2,16,16,896]{3,2,1,0:T(8,128)(2,1)}, s32[8,512]{1,0:T(8,128)}, f32[8,128]{1,0:T(8,128)}) custom-call(s32[4,512]{1,0:T(4,128)} %token_ids_ref.1, s32[4,512]{1,0:T(4,128)} %next_ids_ref.1, bf16[128,896]{1,0:T(8,128)(2,1)} %bitcast.21, bf16[128,896]{1,0:T(8,128)(2,1)} %bitcast.23, f32[1,7168]{1,0:T(1,128)} %gain_ref.1, ...), custom_call_target="tpu_custom_call" | custom-call | tf_op jit(solution)/shard_map/train_step_32/pallas_call | solution.py:997
  128.8 1.2 slice.3
  130.6 0.0 copy-done
  130.6 0.0 copy-done.2
  130.7 0.0 copy-done.3
  130.7 4.8 %conditional.1 = (bf16[2048,896]{1,0:T(8,128)(2,1)S(1)}) conditional(s32[]{:T(128)} %bitcast.12, (bf16[4,32,896]{2,1,0:T(8,128)(2,1)S(1)}, bf16[4,32,896]{2,1,0:T(8,128)(2,1)S(1)}, bf16[1,7168,128]{2,1,0:T(8,128)(2,1)}, bf16[1,7168,128]{2,1,0:T(8,128)(2,1)}, bf16[1,128,7168]{2,1,0:T(8,128)(2,1)}, /*index=5*/s32[4,512]{1,0:T(4,128)}, ...), branch_computations={%region_0.0_spmd, %region_1.0_spmd} | conditional | bytes 8 | solution.py:1110
  130.7 4.8 %place_rows.3 = bf16[2048,896]{1,0:T(8,128)(2,1)S(1)} custom-call(s32[8,512]{1,0:T(8,128)} %get-tuple-element.44.lid_ref, bf16[512,896]{1,0:T(8,128)(2,1)} %bitcast.20), custom_call_target="tpu_custom_call" | custom-call | tf_op jit(solution)/shard_map/cond/branch_1_fun/place_rows/pallas_call | solution.py:1084
  135.5 0.0 copy-start.1
  135.5 1.8 %copy-done.1 = bf16[2048,896]{1,0:T(8,128)(2,1)} copy-done((bf16[2048,896]{1,0:T(8,128)(2,1)}, bf16[2048,896]{1,0:T(8,128)(2,1)S(1)}, u32[]{:S(2)}) %copy-start.1) | copy-done | bytes 3670040
Async XLA Ops:
  0.0 130.6 %copy-start = (bf16[2048,896]{1,0:T(8,128)(2,1)S(1)}, bf16[2048,896]{1,0:T(8,128)(2,1)}, u32[]{:S(2)}) copy-start(bf16[2048,896]{1,0:T(8,128)(2,1)} %table_hbm.1) | copy-start | bytes 11010052
  0.0 130.6 %copy-start.2 = (bf16[4,32,896]{2,1,0:T(8,128)(2,1)S(1)}, bf16[4,32,896]{2,1,0:T(8,128)(2,1)}, u32[]{:S(2)}) copy-start(bf16[4,32,896]{2,1,0:T(8,128)(2,1)} %param.20) | copy-start | bytes 688132
  0.0 130.7 %copy-start.3 = (bf16[4,32,896]{2,1,0:T(8,128)(2,1)S(1)}, bf16[4,32,896]{2,1,0:T(8,128)(2,1)}, u32[]{:S(2)}) copy-start(bf16[4,32,896]{2,1,0:T(8,128)(2,1)} %param.21) | copy-start | bytes 688132
  135.5 1.8 %copy-start.1 = (bf16[2048,896]{1,0:T(8,128)(2,1)}, bf16[2048,896]{1,0:T(8,128)(2,1)S(1)}, u32[]{:S(2)}) copy-start(bf16[2048,896]{1,0:T(8,128)(2,1)S(1)} %get-tuple-element.55) | copy-start | bytes 11010052
